TPU v7x, 256 devices: a whole 4x4x8 slice. The times are simulated.
256 devices in a mesh: dp: 64 (over z, x, core), replica: 4 (over y).
Axes of the slice: x: 4, y: 4, z: 8, core: 2. Of those that a mesh axis runs over, the one named last changes fastest.
Arguments:
- gradients: bfloat16 [56, 1024, 1024], P(None, 'dp', 'replica')
- adagrad: float32 [56, 1024, 1024], P(None, 'dp', 'replica'), may hold values from 0.003 to 0.03
- factor_left: float32 [128, 1024, 1024], P('dp', 'replica'), may hold values from -4 to 4
- factor_right: float32 [128, 1024, 1024], P('dp', 'replica'), may hold values from -4 to 4
- root_left: bfloat16 [128, 1024, 1024], P('dp', 'replica')
- root_right: bfloat16 [128, 1024, 1024], P('dp', None, 'replica')
- block_slot: int32 [56], replicated, may hold values from 0 to 127, as said below
Outputs:
- update: bfloat16 [56, 1024, 1024], P(None, 'dp', 'replica')
- adagrad_new: float32 [56, 1024, 1024], P(None, 'dp', 'replica')
- factor_left_new: float32 [128, 1024, 1024], P('dp', 'replica')
- factor_right_new: float32 [128, 1024, 1024], P('dp', 'replica')
Inputs may be any that keep to these rules, and one draw needn't show every extreme that they name: block_slot holds distinct slot numbers; slot t belongs to owner group t // 2, so an owner group serves 0 to 2 blocks.
All inputs are finite; a program needn't handle non-finite values.
Results may differ from a plain program's by a relative error of at most 0.0058.
Values may be sent and summed in bfloat16 or wider, within the bound.
A program may use at most 64 MiB of HBM per device.

v0:
```python
import jax
import jax.numpy as jnp
from jax import lax
from jax.sharding import PartitionSpec as P


def to_blocks(values, placing, n_dp, rows, cols):
    count = values.shape[0]
    arrived = lax.all_to_all(
        values.reshape(count, n_dp, rows, cols), "dp", split_axis=1, concat_axis=1, tiled=True
    )
    flat = arrived.reshape(count * n_dp, rows * cols)
    return lax.dot_general(
        placing, flat, (((0,), (0,)), ((), ())), preferred_element_type=jnp.float32
    )


def on_device(gradients, adagrad, factor_left, factor_right, root_left, root_right, block_slot):
    n_dp = lax.axis_size("dp")
    count = factor_left.shape[0]
    nblk, rows, cols = gradients.shape
    width = rows * n_dp
    slot_grid = (
        jnp.arange(count, dtype=jnp.int32)[:, None]
        + count * jnp.arange(n_dp, dtype=jnp.int32)[None, :]
    )
    placing = (slot_grid.reshape(-1)[:, None] == block_slot[None, :]).astype(jnp.bfloat16)
    flat_grads = gradients.reshape(nblk, rows * cols)
    outgoing = jnp.dot(placing, flat_grads, preferred_element_type=jnp.float32).astype(jnp.bfloat16)
    columns = lax.all_to_all(
        outgoing.reshape(count, n_dp, rows, cols), "dp", split_axis=1, concat_axis=1, tiled=True
    ).reshape(count, width, cols)
    grads32 = gradients.astype(jnp.float32).reshape(nblk, rows * cols)
    adagrad_new = adagrad.reshape(nblk, rows * cols) + grads32 * grads32
    scaled = grads32 / (jnp.sqrt(adagrad_new) + 1e-08)
    graft_part = jnp.sum(scaled * scaled, axis=1)
    full = lax.all_gather(columns, "replica", axis=2, tiled=True)
    own_rows = lax.dynamic_slice_in_dim(full, lax.axis_index("replica") * cols, cols, 1)
    left_term = jnp.einsum("sij,skj->sik", own_rows, full, preferred_element_type=jnp.float32)
    right_term = jnp.einsum("sji,sjk->sik", columns, full, preferred_element_type=jnp.float32)
    factor_left_new = 0.9 * factor_left + 0.1 * left_term
    factor_right_new = 0.9 * factor_right + 0.1 * right_term
    half_rows = jnp.einsum(
        "sij,sjk->sik", root_left, full, preferred_element_type=jnp.float32
    ).astype(jnp.bfloat16)
    search_cols = jnp.einsum(
        "sij,sjk->sik",
        lax.all_gather(half_rows, "replica", axis=1, tiled=True),
        root_right,
        preferred_element_type=jnp.float32,
    ).astype(jnp.bfloat16)
    search_local = to_blocks(search_cols, placing, n_dp, rows, cols)
    search_part = jnp.sum(search_local * search_local, axis=1)
    graft_sq, search_sq = lax.psum((graft_part, search_part), ("dp", "replica"))
    ratio = jnp.sqrt(graft_sq) / (jnp.sqrt(search_sq) + 1e-06)
    update = (search_local * ratio[:, None]).astype(jnp.bfloat16)
    return (
        update.reshape(nblk, rows, cols),
        adagrad_new.reshape(nblk, rows, cols),
        factor_left_new,
        factor_right_new,
    )


def solution(mesh):
    placed = (
        P(None, "dp", "replica"),
        P(None, "dp", "replica"),
        P("dp", "replica", None),
        P("dp", "replica", None),
        P("dp", "replica", None),
        P("dp", None, "replica"),
        P(),
    )
    return jax.shard_map(
        on_device,
        mesh=mesh,
        in_specs=placed,
        out_specs=(
            P(None, "dp", "replica"),
            P(None, "dp", "replica"),
            P("dp", "replica", None),
            P("dp", "replica", None),
        ),
        check_vma=False,
    )
```

profile of v0, /device:TPU:9, one launch (start us, length us, event | category | flops | bytes accessed | tf_op | source)
XLA Modules:
  0.0 285.4 jit_solution(15204427737320641448)
XLA Ops:
  7.2 0.1 add.54
  7.3 1.3 copy.39
  8.6 1.1 convolution_convert_fusion
  9.7 0.2 copy.40
  10.0 0.1 copy.24
  10.1 39.9 %all_to_all.10 = bf16[2,64,16,256]{3,2,0,1:T(8,128)(2,1)S(1)} all-to-all(bf16[2,64,16,256]{3,2,0,1:T(8,128)(2,1)S(1)} %copy.24), channel_id=1, replica_groups=mesh['dp'=64,'replica'=4] {'dp'}, dimensions={1} | all-to-all | bytes 2097152 | tf_op jit(solution)/shard_map/all_to_all | solution.py:30
  50.1 0.1 copy.25
  50.1 1.3 copy.26
  51.6 47.5 %all-gather.3.cloned.1.call-done = bf16[2,1024,1024]{1,2,0:T(8,128)(2,1)} async-done(((bf16[2,1024,256]{1,2,0:T(8,128)(2,1)}), bf16[2,1024,1024]{1,2,0:T(8,128)(2,1)}) %all-gather.3.cloned.1.call-update) | async-done | bytes 4194320 | tf_op jit(solution)/shard_map/all_gather | solution.py:37
  99.0 4.5 %fusion = bf16[2,256,1024]{1,2,0:T(8,128)(2,1)} fusion(bf16[2,1024,1024]{1,2,0:T(8,128)(2,1)} %all-gather.3.cloned.1.call-done, bf16[2,256,1024]{2,1,0:T(8,128)(2,1)S(1)} %copy-done), kind=kOutput, calls=%fused_computation.5 | convolution fusion | flops 1074266112 | bytes 6291456 | tf_op jit(solution)/shard_map/sij,sjk->sik/dot_general | solution.py:43
  103.5 54.1 %all-gather.5.cloned.1.call-done = bf16[2,1024,1024]{1,2,0:T(8,128)(2,1)} async-done(((bf16[2,256,1024]{1,2,0:T(8,128)(2,1)}), bf16[2,1024,1024]{1,2,0:T(8,128)(2,1)}) %all-gather.5.cloned.1.call-update) | async-done | bytes 4194320 | tf_op jit(solution)/shard_map/all_gather | solution.py:48
  157.6 3.9 %convolution_convert_fusion.1 = bf16[2,1024,256]{2,1,0:T(8,128)(2,1)S(1)} fusion(bf16[2,1024,1024]{1,2,0:T(8,128)(2,1)} %all-gather.5.cloned.1.call-done, bf16[2,1024,256]{2,1,0:T(8,128)(2,1)S(1)} %copy-done.5), kind=kOutput, calls=%fused_computation.3 | convolution fusion | flops 1074266112 | bytes 6291456 | tf_op jit(solution)/shard_map/sij,sjk->sik/dot_general | solution.py:46
  161.5 1.1 copy.28
  162.6 11.5 %all-to-all-start.1 = ((bf16[2,64,16,256]{3,2,0,1:T(8,128)(2,1)}), bf16[2,64,16,256]{3,2,0,1:T(8,128)(2,1)S(1)}, u32[]{:S(2)}, u32[]{:S(2)}) async-start(bf16[2,64,16,256]{3,2,0,1:T(8,128)(2,1)} %copy.28), calls=%async_computation.1 | async-start | bytes 2097152 | tf_op jit(solution)/shard_map/all_to_all | solution.py:9
  174.2 2.9 %fusion.4 = (f32[56]{0:T(128)S(1)}, f32[56,16,256]{2,1,0:T(8,128)}) fusion(bf16[56,16,256]{2,1,0:T(8,128)(2,1)} %param.7, f32[56,16,256]{2,1,0:T(8,128)} %param.8), kind=kLoop, calls=%fused_computation.13 | loop fusion | flops 1605576 | bytes 2293984 | tf_op jit(solution)/shard_map/reduce_sum | solution.py:36
  177.1 5.5 %multiply_add_fusion.1 = f32[2,256,1024]{2,1,0:T(8,128)} fusion(f32[2,256,1024]{2,1,0:T(8,128)S(1)} %copy-done.2, bf16[2,1024,1024]{1,2,0:T(8,128)(2,1)} %all-gather.3.cloned.1.call-done, s32[]{:T(128)S(6)} %select_n.3), kind=kOutput, calls=%fused_computation.2 | convolution fusion | flops 1075314688 | bytes 9437188 | tf_op jit(solution)/shard_map/sij,skj->sik/dot_general | solution.py:39
  182.6 3.2 %multiply_add_fusion = f32[2,256,1024]{2,1,0:T(8,128)} fusion(f32[2,256,1024]{2,1,0:T(8,128)S(1)} %copy-done.3, bf16[2,1024,256]{2,1,0:T(8,128)(2,1)S(1)} %bitcast.24, bf16[2,1024,1024]{1,2,0:T(8,128)(2,1)S(1)} %copy-done.1), kind=kOutput, calls=%fused_computation.1 | convolution fusion | flops 1075314688 | bytes 9437184 | tf_op jit(solution)/shard_map/sji,sjk->sik/dot_general | solution.py:40
  185.8 16.3 %all-to-all-done.1 = bf16[2,64,16,256]{3,2,0,1:T(8,128)(2,1)S(1)} async-done(((bf16[2,64,16,256]{3,2,0,1:T(8,128)(2,1)}), bf16[2,64,16,256]{3,2,0,1:T(8,128)(2,1)S(1)}, u32[]{:S(2)}, u32[]{:S(2)}) %all-to-all-start.1) | async-done | bytes 1048608 | tf_op jit(solution)/shard_map/all_to_all | solution.py:9
  202.1 0.1 copy.29
  202.2 0.4 copy.41
  202.7 0.5 multiply_reduce_fusion
  203.2 74.4 %all-reduce = (f32[56]{0:T(128)S(1)}, f32[56]{0:T(128)S(1)}) all-reduce(f32[56]{0:T(128)S(1)} %get-tuple-element.8, f32[56]{0:T(128)S(1)} %get-tuple-element.6), channel_id=1, replica_groups=mesh['dp'=64,'replica'=4] {'dp','replica'}, use_global_device_ids=true, to_apply=%region_3.0 | all-reduce | flops 112 | bytes 896 | tf_op jit(solution)/shard_map/psum | solution.py:54
  277.6 0.1 multiply_convert_fusion
  277.7 0.9 copy.42
  (19 shorter events, 0.2 us)
Async XLA Ops:
  7.2 91.9 %copy-start = (bf16[2,256,1024]{2,1,0:T(8,128)(2,1)S(1)}, bf16[2,256,1024]{2,1,0:T(8,128)(2,1)}, u32[]{:S(2)}) copy-start(bf16[2,256,1024]{2,1,0:T(8,128)(2,1)} %param.11) | copy-start | bytes 3145732
  7.2 91.8 %all-gather.3.cloned.1.call-start = ((), (), s32[]{:S(2)}) async-start(), calls=%async_computation.2 | async-start | bytes 5242880 | tf_op jit(solution)/shard_map/all_gather | solution.py:37
  51.5 106.1 %copy-start.5 = (bf16[2,1024,256]{2,1,0:T(8,128)(2,1)S(1)}, bf16[2,1024,256]{2,1,0:T(8,128)(2,1)}, u32[]{:S(2)}) copy-start(bf16[2,1024,256]{2,1,0:T(8,128)(2,1)} %param.12) | copy-start | bytes 3145732
  51.5 106.1 %all-gather.5.cloned.1.call-start = ((), (), s32[]{:S(2)}) async-start(), calls=%async_computation.3 | async-start | bytes 5242880 | tf_op jit(solution)/shard_map/all_gather | solution.py:48
  162.6 39.5 %all-to-all-start.1 = ((bf16[2,64,16,256]{3,2,0,1:T(8,128)(2,1)}), bf16[2,64,16,256]{3,2,0,1:T(8,128)(2,1)S(1)}, u32[]{:S(2)}, u32[]{:S(2)}) async-start(bf16[2,64,16,256]{3,2,0,1:T(8,128)(2,1)} %copy.28), calls=%async_computation.1 | async-start | bytes 2097152 | tf_op jit(solution)/shard_map/all_to_all | solution.py:9
  174.1 3.0 %copy-start.2 = (f32[2,256,1024]{2,1,0:T(8,128)S(1)}, f32[2,256,1024]{2,1,0:T(8,128)}, u32[]{:S(2)}) copy-start(f32[2,256,1024]{2,1,0:T(8,128)} %param.9) | copy-start | bytes 6291460
  177.1 5.5 %copy-start.1 = (bf16[2,1024,1024]{1,2,0:T(8,128)(2,1)S(1)}, bf16[2,1024,1024]{1,2,0:T(8,128)(2,1)}, u32[]{:S(2)}) copy-start(bf16[2,1024,1024]{1,2,0:T(8,128)(2,1)} %all-gather.3.cloned.1.call-done) | copy-start | bytes 12582916
  177.1 5.5 %copy-start.3 = (f32[2,256,1024]{2,1,0:T(8,128)S(1)}, f32[2,256,1024]{2,1,0:T(8,128)}, u32[]{:S(2)}) copy-start(f32[2,256,1024]{2,1,0:T(8,128)} %param.10) | copy-start | bytes 6291460
  185.8 16.8 %copy-start.4 = (s32[56]{0:T(128)S(1)}, s32[56]{0:T(128)}, u32[]{:S(2)}) copy-start(s32[56]{0:T(128)} %param.13) | copy-start | bytes 676
Sparse Core Ops, SparseCore 0:
  51.6 47.3 all-gather.2
  103.6 53.9 all-gather.4
where the time goes:
time: 288 us; the launch traced here: 285 us
  waiting for transfers between devices  118 us (41%)
  blocking collectives  114 us (40%)
  matrix products  18.7 us (6%)
  between operations  14.2 us (5%)
  starting transfers between devices  11.6 us (4%)
  local copies, waits for them, and re-layouts  5.59 us (2%)
  other arithmetic  3.09 us (1%)
    psum x1, blocking collectives, on_device(): graft_sq, search_sq = lax.psum((graft_part, search_part), ('dp', 'replica'))  74.4 us
    all_gather x1, waiting for transfers between devices, on_device(): lax.all_gather(half_rows, 'replica', axis=1, tiled=True)  54.1 us
    all_gather x1, waiting for transfers between devices, on_device(): full = lax.all_gather(columns, 'replica', axis=2, tiled=True)  47.5 us
    all_to_all x1, blocking collectives, on_device(): lax.all_to_all(outgoing.reshape(count, n_dp, rows, cols), 'dp', split_axi...  39.9 us
    all_to_all x1, waiting for transfers between devices, to_blocks(): lax.all_to_all(values.reshape(count, n_dp, rows, cols), 'dp', split_axis=...  16.3 us
    all_to_all x1, starting transfers between devices, to_blocks(): lax.all_to_all(values.reshape(count, n_dp, rows, cols), 'dp', split_axis=...  11.5 us
  transfers between devices with their start and end apart: 3, of which 3 were waited for; matrix products, arithmetic and copies ran while one was open for 4% of the time, Pallas kernels for 0%

commit v1 on v0

v1 whole, which is shorter than its diff:
```python
import jax
import jax.numpy as jnp
from jax import lax
from jax.experimental import pallas as pl
from jax.experimental.pallas import tpu as pltpu
from jax.sharding import PartitionSpec as P

MESH = pl.DeviceIdType.MESH
NZ, NX, NC, NY = 8, 4, 2, 4
ROWS, COLS, WIDTH = 16, 256, 1024
SLOTS = NZ * NX * NY
NBLK = 56
F32, BF16 = jnp.float32, jnp.bfloat16


def device(z, x, core, y):
    return (z * (NX * NC) + x * NC + core, y)


def drain(ref, sem):
    pltpu.make_async_copy(ref, ref, sem).wait()


def kernel(
    slot_ref, inv_ref, g_ref, a_ref, rl_ref, rr_ref,
    upd_ref, left_ref, right_ref,
    sbuf, gbuf, rlb, rrb, hb, sb, ubr, lb, rb, gp, ar_z, ar_x, ar_y, ar_c,
    g_send, g_recv, gx_send, gx_recv, rl_send, rl_recv, rr_send, rr_recv,
    rx_send, rx_recv, f_send, f_recv, u_send, u_recv,
    z_send, z_recv, x_send, x_recv, y_send, y_recv, c_send, c_recv,
):
    d = lax.axis_index("dp")
    y = lax.axis_index("replica")
    z, x, core = d // (NX * NC), (d // NC) % NX, d % NC
    other = 1 - core
    zx = z * NX + x
    mine = zx * NY + y
    partner = device(z, x, other, y)

    def target(k):
        return (z + k % NZ) % NZ, (x + (k // NZ) % NX) % NX, (y + k // (NZ * NX)) % NY

    def remote(src, dst, send, recv, where):
        return pltpu.make_async_remote_copy(
            src_ref=src, dst_ref=dst, send_sem=send, recv_sem=recv,
            device_id=where, device_id_type=MESH,
        )

    barrier = pltpu.get_barrier_semaphore()

    def greet(k, _):
        tz, tx, ty = target(k)
        pl.semaphore_signal(barrier, inc=1, device_id=device(tz, tx, core, ty), device_id_type=MESH)
        return 0

    lax.fori_loop(1, SLOTS, greet, 0)
    for ty in range(NY):
        pl.semaphore_signal(barrier, inc=1, device_id=device(z, x, other, ty), device_id_type=MESH)

    def pack(t, _):
        b = inv_ref[t]
        rows = g_ref[jnp.minimum(b, NBLK - 1)]
        sbuf[t] = jnp.where(b < NBLK, rows, jnp.zeros_like(rows))
        return 0

    lax.fori_loop(0, SLOTS, pack, 0)
    pl.semaphore_wait(barrier, SLOTS - 1 + NY)

    def send_rows(k, _):
        tz, tx, ty = target(k)
        remote(
            sbuf.at[(tz * NX + tx) * NY + ty], gbuf.at[y, zx, core],
            g_send, g_recv.at[y], device(tz, tx, core, ty),
        ).start()
        return 0

    own_rows = pltpu.make_async_copy(sbuf.at[mine], gbuf.at[y, zx, core], g_recv.at[y])
    own_rows.start()
    lax.fori_loop(1, SLOTS, send_rows, 0)

    half = WIDTH // 2

    def root_parts(i, q):
        return (
            (rl_ref.at[i, :, q], rlb.at[pl.ds(y * 8, 8)], rl_send.at[i, q], rl_recv),
            (rr_ref.at[i, pl.ds(q * half, half)], rrb.at[y, pl.ds(q * half, half)], rr_send.at[i, q], rr_recv),
        )

    def is_self(i, q):
        return jnp.logical_and(2 * core + i == y, core == q)

    for i in range(2):
        for q in range(NC):
            for src, dst, send, recv in root_parts(i, q):
                @pl.when(is_self(i, q))
                def _(src=src, dst=dst, recv=recv):
                    pltpu.make_async_copy(src, dst, recv).start()

                @pl.when(jnp.logical_not(is_self(i, q)))
                def _(src=src, dst=dst, send=send, recv=recv, i=i, q=q):
                    remote(src, dst, send, recv, device(z, x, q, 2 * core + i)).start()

    gp[...] = jnp.zeros_like(gp)

    def graft(b, _):
        g32 = g_ref[b].astype(F32)
        scaled = g32 / (jnp.sqrt(a_ref[b] + g32 * g32) + 1e-08)
        sq = jnp.sum(scaled * scaled, axis=0, keepdims=True)
        gp[pl.ds(b, 1), :] = sq[:, :128] + sq[:, 128:]
        return 0

    lax.fori_loop(0, NBLK, graft, 0)
    part = jnp.sum(jnp.transpose(gp[...]), axis=0, keepdims=True)
    ar_z[z] = jnp.broadcast_to(part, (8, 128))

    def spread(buf, me, count, send, recv, where):
        copies = []
        for k in range(1, count):
            other_one = (me + k) % count
            copies.append(remote(buf.at[me], buf.at[me], send.at[k], recv.at[k], where(other_one)))
        for cp in copies:
            cp.start()
        return copies

    z_copies = spread(ar_z, z, NZ, z_send, z_recv, lambda o: device(o, x, core, y))

    swaps = []
    for c in range(NY):
        drain(gbuf.at[c, :, core], g_recv.at[c])
        cp = remote(gbuf.at[c, :, core], gbuf.at[c, :, core], gx_send.at[c], gx_recv.at[c], partner)
        cp.start()
        swaps.append(cp)
    for cp in z_copies:
        cp.wait()
    ar_x[x] = jnp.sum(ar_z[...], axis=0)
    x_copies = spread(ar_x, x, NX, x_send, x_recv, lambda o: device(z, o, core, y))
    for cp in swaps:
        cp.wait_recv()

    owner = y // 2
    i_mine = y % 2

    def factor_part(n):
        r = 2 * core + n
        acc = jnp.zeros((COLS, WIDTH), F32)
        for c in range(NY):
            rows = gbuf[c, pl.ds(r * 8, 8)].reshape(COLS, COLS)
            acc = acc + lax.dot_general(
                rows, gbuf[c].reshape(WIDTH, COLS), (((1,), (1,)), ((), ())), preferred_element_type=F32
            )
        lb[n] = acc.astype(BF16)
        cols = gbuf[r].reshape(WIDTH, COLS)
        for c in range(NY):
            rb[n, :, c * COLS:(c + 1) * COLS] = lax.dot_general(
                cols, gbuf[c].reshape(WIDTH, COLS), (((0,), (0,)), ((), ())), preferred_element_type=F32
            ).astype(BF16)

    def factor_self(n):
        return jnp.logical_and(2 * core + n == y, core == owner)

    for n in range(2):
        factor_part(n)
        for m, (src, dst) in enumerate(((lb.at[n], left_ref.at[i_mine]), (rb.at[n], right_ref.at[i_mine]))):
            @pl.when(factor_self(n))
            def _(src=src, dst=dst, m=m):
                pltpu.make_async_copy(src, dst, f_recv.at[m]).start()

            @pl.when(jnp.logical_not(factor_self(n)))
            def _(src=src, dst=dst, m=m, n=n):
                remote(src, dst, f_send.at[n, m], f_recv.at[m], device(z, x, owner, 2 * core + n)).start()

    for cp in x_copies:
        cp.wait()
    ar_y[y] = jnp.sum(ar_x[...], axis=0)
    y_copies = spread(ar_y, y, NY, y_send, y_recv, lambda o: device(z, x, core, o))

    drain(rrb.at[:, pl.ds(core * half, half)], rr_recv)
    rr_swap = remote(
        rrb.at[:, pl.ds(core * half, half)], rrb.at[:, pl.ds(core * half, half)], rx_send, rx_recv, partner
    )
    rr_swap.start()
    drain(rlb, rl_recv)
    rl = rlb[...].reshape(half, WIDTH)
    for c in range(NY):
        hb[:, c * COLS:(c + 1) * COLS] = jnp.dot(
            rl, gbuf[c].reshape(WIDTH, COLS), preferred_element_type=F32
        ).astype(BF16)
    rr_swap.wait_recv()
    sq = jnp.zeros((8, 128), F32)
    for c in range(NY):
        s = jnp.dot(hb[...], rrb[c], preferred_element_type=F32).astype(BF16)
        sb[c] = s.reshape(NZ * NX, ROWS, COLS)
        s32 = s.astype(F32)
        s2 = jnp.sum((s32 * s32).reshape(half // 8, 8, COLS), axis=0)
        sq = sq + s2[:, :128] + s2[:, 128:]
    for cp in y_copies:
        cp.wait()
    ar_c[core, 0] = sq
    ar_c[core, 1] = jnp.sum(ar_y[...], axis=0)
    c_copy = remote(ar_c.at[core], ar_c.at[core], c_send, c_recv, partner)
    c_copy.start()
    c_copy.wait()
    search_sq = jnp.sum(ar_c[0, 0] + ar_c[1, 0], keepdims=True)
    graft_all = ar_c[0, 1, 0:1] + ar_c[1, 1, 0:1]
    lane = lax.broadcasted_iota(jnp.int32, (1, 128), 1)
    graft_sq = jnp.sum(jnp.where(lane == inv_ref[mine], graft_all, 0.0), keepdims=True)
    ratio = jnp.sqrt(graft_sq) / (jnp.sqrt(search_sq) + 1e-06)
    ratio = jnp.broadcast_to(ratio, (1, COLS))

    def scale(k, _):
        for c in range(NY):
            sb[c, k] = (sb[c, k].astype(F32) * ratio).astype(BF16)
        return 0

    lax.fori_loop(0, NZ * NX, scale, 0)

    own_dir = pltpu.make_async_copy(sb.at[y, zx], ubr.at[mine], u_recv)
    own_dir.start()

    def send_dir(k, _):
        tz, tx, ty = target(k)
        remote(
            sb.at[ty, tz * NX + tx], ubr.at[mine], u_send, u_recv, device(tz, tx, core, ty)
        ).start()
        return 0

    lax.fori_loop(1, SLOTS, send_dir, 0)

    drain(ubr, u_recv)

    def pick(b, _):
        upd_ref[b] = ubr[slot_ref[b]]
        return 0

    lax.fori_loop(0, NBLK, pick, 0)

    drain(left_ref, f_recv.at[0])
    drain(right_ref, f_recv.at[1])
    drain(sbuf.at[pl.ds(0, SLOTS - 1)], g_send)
    drain(ubr.at[pl.ds(0, SLOTS - 1)], u_send)
    for cp in swaps:
        cp.wait_send()
    rr_swap.wait_send()
    for i in range(2):
        for q in range(NC):
            @pl.when(jnp.logical_not(is_self(i, q)))
            def _(i=i, q=q):
                for src, dst, send, recv in root_parts(i, q):
                    drain(dst, send)
    for n in range(2):
        @pl.when(jnp.logical_not(factor_self(n)))
        def _(n=n):
            drain(lb.at[n], f_send.at[n, 0])
            drain(rb.at[n], f_send.at[n, 1])


def exchange(block_slot, inverse, gradients, adagrad, root_left, root_right):
    vmem = pl.BlockSpec(memory_space=pltpu.VMEM)
    smem = pl.BlockSpec(memory_space=pltpu.SMEM)
    hbm = pl.BlockSpec(memory_space=pl.ANY)
    dma = pltpu.SemaphoreType.DMA
    return pl.pallas_call(
        kernel,
        out_shape=(
            jax.ShapeDtypeStruct((NBLK, ROWS, COLS), BF16),
            jax.ShapeDtypeStruct((2, COLS, WIDTH), BF16),
            jax.ShapeDtypeStruct((2, COLS, WIDTH), BF16),
        ),
        in_specs=[smem, smem, vmem, vmem, hbm, hbm],
        out_specs=(vmem, hbm, hbm),
        scratch_shapes=[
            pltpu.VMEM((SLOTS, ROWS, COLS), BF16),
            pltpu.VMEM((NY, NZ * NX, NC, ROWS, COLS), BF16),
            pltpu.VMEM((NZ * NX, ROWS, WIDTH), BF16),
            pltpu.VMEM((NY, WIDTH, COLS), BF16),
            pltpu.VMEM((WIDTH // 2, WIDTH), BF16),
            pltpu.VMEM((NY, NZ * NX, ROWS, COLS), BF16),
            pltpu.VMEM((SLOTS, ROWS, COLS), BF16),
            pltpu.VMEM((2, COLS, WIDTH), BF16),
            pltpu.VMEM((2, COLS, WIDTH), BF16),
            pltpu.VMEM((128, 128), F32),
            pltpu.VMEM((NZ, 8, 128), F32),
            pltpu.VMEM((NX, 8, 128), F32),
            pltpu.VMEM((NY, 8, 128), F32),
            pltpu.VMEM((NC, 2, 8, 128), F32),
            dma, dma((NY,)), dma((NY,)), dma((NY,)), dma((2, NC)), dma, dma((2, NC)), dma,
            dma, dma, dma((2, 2)), dma((2,)), dma, dma,
            dma((NZ,)), dma((NZ,)), dma((NX,)), dma((NX,)), dma((NY,)), dma((NY,)), dma, dma,
        ],
        compiler_params=pltpu.CompilerParams(
            collective_id=0, has_side_effects=True, vmem_limit_bytes=48 * 2**20
        ),
        name="shampoo_exchange",
    )(block_slot, inverse, gradients, adagrad, root_left, root_right)


def on_device(gradients, adagrad, factor_left, factor_right, root_left, root_right, block_slot):
    count = factor_left.shape[0]
    numbers = jnp.arange(NBLK, dtype=jnp.int32)
    named = jnp.arange(SLOTS, dtype=jnp.int32)[:, None] == block_slot[None, :]
    inverse = jnp.min(jnp.where(named, numbers[None, :], NBLK), axis=1)
    update, left_term, right_term = exchange(
        block_slot, inverse, gradients, adagrad,
        root_left.reshape(count, 8, NC, ROWS, WIDTH), root_right,
    )
    grads32 = gradients.astype(F32)
    adagrad_new = adagrad + grads32 * grads32
    factor_left_new = 0.9 * factor_left + 0.1 * left_term.astype(F32)
    factor_right_new = 0.9 * factor_right + 0.1 * right_term.astype(F32)
    return update, adagrad_new, factor_left_new, factor_right_new


def solution(mesh):
    placed = (
        P(None, "dp", "replica"),
        P(None, "dp", "replica"),
        P("dp", "replica", None),
        P("dp", "replica", None),
        P("dp", "replica", None),
        P("dp", None, "replica"),
        P(),
    )
    return jax.shard_map(
        on_device,
        mesh=mesh,
        in_specs=placed,
        out_specs=(
            P(None, "dp", "replica"),
            P(None, "dp", "replica"),
            P("dp", "replica", None),
            P("dp", "replica", None),
        ),
        check_vma=False,
    )
```

time: 288 us -> 118 us (0.41)
  waiting for transfers between devices: 118 us -> 0 us
  blocking collectives: 114 us -> 0 us
  Pallas kernels: 0 us -> 103 us
  matrix products: 18.7 us -> 0 us
  between operations: 14.2 us -> 0.66 us
  starting transfers between devices: 11.6 us -> 0 us
  other arithmetic: 3.09 us -> 6.32 us
    pallas_call x0 -> x1, Pallas kernels: none -> 103 us  [exchange(): pl.pallas_call(kernel, out_shape=(jax.ShapeDtypeStruct((NBLK, ROWS, COLS)...]
    all_gather x2 -> x0, waiting for transfers between devices: 102 us -> none  [the longest x1 54.1 us: on_device(): lax.all_gather(half_rows, 'replica', axis=1, tiled=True)]
    psum x1 -> x0, blocking collectives: 74.4 us -> none  [on_device(): graft_sq, search_sq = lax.psum((graft_part, search_part), ('dp', 'replica'))]
    all_to_all x1 -> x0, blocking collectives: 39.9 us -> none  [on_device(): lax.all_to_all(outgoing.reshape(count, n_dp, rows, cols), 'dp', split_axi...]
    dot_general x6 -> x0, matrix products: 18.7 us -> none  [the longest x1 5.47 us: on_device(): jnp.einsum('sij,skj->sik', own_rows, full, preferred_element_type=jnp.flo...]
    all_to_all x1 -> x0, waiting for transfers between devices: 16.3 us -> none  [to_blocks(): lax.all_to_all(values.reshape(count, n_dp, rows, cols), 'dp', split_axis=...]
    all_to_all x1 -> x0, starting transfers between devices: 11.5 us -> none  [to_blocks(): lax.all_to_all(values.reshape(count, n_dp, rows, cols), 'dp', split_axis=...]
    add x1 -> x2, other arithmetic: 0.01 us -> 5.57 us  [the longest x1 4.5 us: on_device(): factor_right_new = 0.9 * factor_right + 0.1 * right_term.astype(F32)]
  transfers between devices with their start and end apart: 3 -> 0, of which waited for: 3 -> 0; matrix products, arithmetic and copies ran while one was open for 4% -> 0% of each run, Pallas kernels for 0% -> 0%
where the time goes in v1:
time: 118 us; the launch traced here: 116 us
  Pallas kernels  103 us (87%)
  other arithmetic  6.32 us (5%)
  local copies, waits for them, and re-layouts  6.07 us (5%)
    pallas_call x1, Pallas kernels, exchange(): pl.pallas_call(kernel, out_shape=(jax.ShapeDtypeStruct((NBLK, ROWS, COLS)...  103 us
    unnamed x13, local copies, waits for them, and re-layouts  6.07 us
    add x1, other arithmetic, on_device(): factor_right_new = 0.9 * factor_right + 0.1 * right_term.astype(F32)  4.5 us

profile of v1, /device:TPU:9, one launch (start us, length us, event | category | flops | bytes accessed | tf_op | source)
XLA Modules:
  0.0 116.4 jit_solution(16128328239684165338)
XLA Ops:
  0.6 0.7 select_reduce_fusion.inv_ref
  1.4 0.0 copy-start
  1.4 1.2 %copy-done = f32[56,16,256]{2,1,0:T(8,128)S(1)} copy-done((f32[56,16,256]{2,1,0:T(8,128)S(1)}, f32[56,16,256]{2,1,0:T(8,128)}, u32[]{:S(2)}) %copy-start) | copy-done | bytes 917528
  2.6 0.0 copy-start.1
  2.6 1.0 copy-done.1
  3.6 0.0 copy-start.2
  3.6 1.2 %copy-done.2 = bf16[2,256,1024]{2,1,0:T(8,128)(2,1)S(1)} copy-done((bf16[2,256,1024]{2,1,0:T(8,128)(2,1)S(1)}, bf16[2,256,1024]{2,1,0:T(8,128)(2,1)}, u32[]{:S(2)}) %copy-start.2) | copy-done | bytes 1048600
  4.8 0.0 copy-start.3
  4.8 1.2 %copy-done.3 = bf16[2,1024,256]{2,1,0:T(8,128)(2,1)S(1)} copy-done((bf16[2,1024,256]{2,1,0:T(8,128)(2,1)S(1)}, bf16[2,1024,256]{2,1,0:T(8,128)(2,1)}, u32[]{:S(2)}) %copy-start.3) | copy-done | bytes 1048600
  6.0 0.0 copy-start.4
  6.0 0.7 copy-done.4
  6.7 0.0 copy-start.5
  6.7 103.3 %shampoo_exchange.1 = (bf16[56,16,256]{2,1,0:T(8,128)(2,1)S(1)}, bf16[2,256,1024]{2,1,0:T(8,128)(2,1)S(1)}, bf16[2,256,1024]{2,1,0:T(8,128)(2,1)S(1)}) custom-call(s32[56]{0:T(128)S(1)} %copy-done.4, s32[128]{0:T(128)S(1)} %select_reduce_fusion.inv_ref, bf16[56,16,256]{2,1,0:T(8,128)(2,1)S(1)} %copy-done.1, f32[56,16,256]{2,1,0:T(8,128)S(1)} %copy-done, ...), custom_call_target="tpu_custom_call" | custom-call | tf_op jit(solution)/shard_map/shampoo_exchange/pallas_call | solution.py:262
  110.0 0.0 copy-done.5
  110.0 4.5 %multiply_add_fusion = (f32[2,256,1024]{2,1,0:T(8,128)}, f32[2,256,1024]{2,1,0:T(8,128)}) fusion(bf16[2,256,1024]{2,1,0:T(8,128)(2,1)S(1)} %get-tuple-element.9, f32[2,256,1024]{2,1,0:T(8,128)S(1)} %copy-done.5, bf16[2,256,1024]{2,1,0:T(8,128)(2,1)S(1)} %get-tuple-element.8, f32[2,256,1024]{2,1,0:T(8,128)} %param.9), kind=kLoop, calls=%fused_computation | loop fusion | flops 4194304 | bytes 10485760 | tf_op jit(solution)/shard_map/add | solution.py:309
  114.6 1.1 multiply_add_fusion.2
  115.6 0.8 copy.12
Async XLA Ops:
  1.4 1.2 %copy-start = (f32[56,16,256]{2,1,0:T(8,128)S(1)}, f32[56,16,256]{2,1,0:T(8,128)}, u32[]{:S(2)}) copy-start(f32[56,16,256]{2,1,0:T(8,128)} %a_ref.1) | copy-start | bytes 2752516
  2.6 1.0 copy-start.1
  3.6 1.2 %copy-start.2 = (bf16[2,256,1024]{2,1,0:T(8,128)(2,1)S(1)}, bf16[2,256,1024]{2,1,0:T(8,128)(2,1)}, u32[]{:S(2)}) copy-start(bf16[2,256,1024]{2,1,0:T(8,128)(2,1)} %param.11) | copy-start | bytes 3145732
  4.8 1.2 %copy-start.3 = (bf16[2,1024,256]{2,1,0:T(8,128)(2,1)S(1)}, bf16[2,1024,256]{2,1,0:T(8,128)(2,1)}, u32[]{:S(2)}) copy-start(bf16[2,1024,256]{2,1,0:T(8,128)(2,1)} %rr_ref.1) | copy-start | bytes 3145732
  6.0 0.7 copy-start.4
  6.7 103.4 %copy-start.5 = (f32[2,256,1024]{2,1,0:T(8,128)S(1)}, f32[2,256,1024]{2,1,0:T(8,128)}, u32[]{:S(2)}) copy-start(f32[2,256,1024]{2,1,0:T(8,128)} %param.10) | copy-start | bytes 6291460

commit v2 on v1

--- a/solution.py
+++ b/solution.py
@@ -22,10 +22,10 @@
 
 
 def kernel(
-    slot_ref, inv_ref, g_ref, a_ref, rl_ref, rr_ref,
+    slot_ref, inv_ref, g_hbm, a_hbm, rl_ref, rr_ref,
     upd_ref, left_ref, right_ref,
-    sbuf, gbuf, rlb, rrb, hb, sb, ubr, lb, rb, gp, ar_z, ar_x, ar_y, ar_c,
-    g_send, g_recv, gx_send, gx_recv, rl_send, rl_recv, rr_send, rr_recv,
+    g_ref, a_ref, in_sem, meet, sbuf, gbuf, rlb, rrb, hb, sb, ubr, lb, rb, gp, ar_z, ar_x, ar_y, ar_c,
+    g_send, g_recv, gx_send, gx_recv, root_send, root_recv,
     rx_send, rx_recv, f_send, f_recv, u_send, u_recv,
     z_send, z_recv, x_send, x_recv, y_send, y_recv, c_send, c_recv,
 ):
@@ -38,7 +38,8 @@
     partner = device(z, x, other, y)
 
     def target(k):
-        return (z + k % NZ) % NZ, (x + (k // NZ) % NX) % NX, (y + k // (NZ * NX)) % NY
+        m = (k * 37) % SLOTS
+        return (z + m % NZ) % NZ, (x + (m // NZ) % NX) % NX, (y + m // (NZ * NX)) % NY
 
     def remote(src, dst, send, recv, where):
         return pltpu.make_async_remote_copy(
@@ -46,16 +47,24 @@
             device_id=where, device_id_type=MESH,
         )
 
+    loads = [
+        pltpu.make_async_copy(g_hbm, g_ref, in_sem.at[0]),
+        pltpu.make_async_copy(a_hbm, a_ref, in_sem.at[1]),
+    ]
+    for cp in loads:
+        cp.start()
+
+    along_z = [device((z + k) % NZ, x, core, y) for k in range(1, NZ)]
+    along_x = [device(z, (x + k) % NX, core, y) for k in range(1, NX)]
+    along_y = [device(z, x, core, (y + k) % NY) for k in range(1, NY)]
     barrier = pltpu.get_barrier_semaphore()
 
-    def greet(k, _):
-        tz, tx, ty = target(k)
-        pl.semaphore_signal(barrier, inc=1, device_id=device(tz, tx, core, ty), device_id_type=MESH)
-        return 0
-
-    lax.fori_loop(1, SLOTS, greet, 0)
-    for ty in range(NY):
-        pl.semaphore_signal(barrier, inc=1, device_id=device(z, x, other, ty), device_id_type=MESH)
+    def greet(sem, devices):
+        for one in devices:
+            pl.semaphore_signal(sem, inc=1, device_id=one, device_id_type=MESH)
+
+    first = along_z + along_x + along_y + [partner]
+    greet(barrier, first)
 
     def pack(t, _):
         b = inv_ref[t]
@@ -63,42 +72,54 @@
         sbuf[t] = jnp.where(b < NBLK, rows, jnp.zeros_like(rows))
         return 0
 
+    loads[0].wait()
     lax.fori_loop(0, SLOTS, pack, 0)
-    pl.semaphore_wait(barrier, SLOTS - 1 + NY)
-
-    def send_rows(k, _):
+    pl.semaphore_wait(barrier, len(first))
+    greet(meet.at[0], along_y)
+    pl.semaphore_wait(meet.at[0], len(along_y))
+    greet(meet.at[1], along_x)
+    pl.semaphore_wait(meet.at[1], len(along_x))
+
+    half = WIDTH // 2
+    own_rows = pltpu.make_async_copy(sbuf.at[mine], gbuf.at[y, zx, core], g_recv.at[y])
+    own_rows.start()
+
+    def send_rows(k):
         tz, tx, ty = target(k)
         remote(
             sbuf.at[(tz * NX + tx) * NY + ty], gbuf.at[y, zx, core],
             g_send, g_recv.at[y], device(tz, tx, core, ty),
         ).start()
-        return 0
-
-    own_rows = pltpu.make_async_copy(sbuf.at[mine], gbuf.at[y, zx, core], g_recv.at[y])
-    own_rows.start()
-    lax.fori_loop(1, SLOTS, send_rows, 0)
-
-    half = WIDTH // 2
-
-    def root_parts(i, q):
-        return (
-            (rl_ref.at[i, :, q], rlb.at[pl.ds(y * 8, 8)], rl_send.at[i, q], rl_recv),
-            (rr_ref.at[i, pl.ds(q * half, half)], rrb.at[y, pl.ds(q * half, half)], rr_send.at[i, q], rr_recv),
-        )
 
     def is_self(i, q):
         return jnp.logical_and(2 * core + i == y, core == q)
 
-    for i in range(2):
-        for q in range(NC):
-            for src, dst, send, recv in root_parts(i, q):
-                @pl.when(is_self(i, q))
-                def _(src=src, dst=dst, recv=recv):
-                    pltpu.make_async_copy(src, dst, recv).start()
-
-                @pl.when(jnp.logical_not(is_self(i, q)))
-                def _(src=src, dst=dst, send=send, recv=recv, i=i, q=q):
-                    remote(src, dst, send, recv, device(z, x, q, 2 * core + i)).start()
+    def send_root(i, q, m, n):
+        if m == 0:
+            src, dst = rl_ref.at[i, n, q], rlb.at[y * 8 + n]
+        else:
+            rows = pl.ds(pl.multiple_of(q * half + n * (half // 8), half // 8), half // 8)
+            src, dst = rr_ref.at[i, rows], rrb.at[y, rows]
+
+        @pl.when(is_self(i, q))
+        def _():
+            pltpu.make_async_copy(src, dst, root_recv.at[m]).start()
+
+        @pl.when(jnp.logical_not(is_self(i, q)))
+        def _():
+            remote(src, dst, root_send.at[m, i, q], root_recv.at[m], device(z, x, q, 2 * core + i)).start()
+
+    def send_all(n, _):
+        for u, (i, q, m) in enumerate([(i, q, m) for i in range(2) for q in range(NC) for m in range(2)]):
+            @pl.when(n * 16 + 2 * u > 0)
+            def _(u=u):
+                send_rows(n * 16 + 2 * u)
+
+            send_root(i, q, m, n)
+            send_rows(n * 16 + 2 * u + 1)
+        return 0
+
+    lax.fori_loop(0, 8, send_all, 0)
 
     gp[...] = jnp.zeros_like(gp)
 
@@ -109,6 +130,7 @@
         gp[pl.ds(b, 1), :] = sq[:, :128] + sq[:, 128:]
         return 0
 
+    loads[1].wait()
     lax.fori_loop(0, NBLK, graft, 0)
     part = jnp.sum(jnp.transpose(gp[...]), axis=0, keepdims=True)
     ar_z[z] = jnp.broadcast_to(part, (8, 128))
@@ -140,7 +162,7 @@
     owner = y // 2
     i_mine = y % 2
 
-    def factor_part(n):
+    def left_part(n):
         r = 2 * core + n
         acc = jnp.zeros((COLS, WIDTH), F32)
         for c in range(NY):
@@ -148,38 +170,52 @@
             acc = acc + lax.dot_general(
                 rows, gbuf[c].reshape(WIDTH, COLS), (((1,), (1,)), ((), ())), preferred_element_type=F32
             )
-        lb[n] = acc.astype(BF16)
-        cols = gbuf[r].reshape(WIDTH, COLS)
+        lb[n] = acc.astype(BF16).reshape(ROWS, ROWS, WIDTH)
+
+    def right_part(n):
+        cols = gbuf[2 * core + n].reshape(WIDTH, COLS)
         for c in range(NY):
-            rb[n, :, c * COLS:(c + 1) * COLS] = lax.dot_general(
+            rb[n, :, :, c * COLS:(c + 1) * COLS] = lax.dot_general(
                 cols, gbuf[c].reshape(WIDTH, COLS), (((0,), (0,)), ((), ())), preferred_element_type=F32
-            ).astype(BF16)
+            ).astype(BF16).reshape(ROWS, ROWS, COLS)
 
     def factor_self(n):
         return jnp.logical_and(2 * core + n == y, core == owner)
 
+    def send_factor(m, n, piece):
+        src = (lb, rb)[m].at[n, piece]
+        dst = (left_ref, right_ref)[m].at[i_mine, piece]
+
+        @pl.when(factor_self(n))
+        def _():
+            pltpu.make_async_copy(src, dst, f_recv.at[m]).start()
+
+        @pl.when(jnp.logical_not(factor_self(n)))
+        def _():
+            remote(src, dst, f_send.at[m, n], f_recv.at[m], device(z, x, owner, 2 * core + n)).start()
+
+    def send_left(piece, _):
+        for n in range(2):
+            send_factor(0, n, piece)
+        return 0
+
     for n in range(2):
-        factor_part(n)
-        for m, (src, dst) in enumerate(((lb.at[n], left_ref.at[i_mine]), (rb.at[n], right_ref.at[i_mine]))):
-            @pl.when(factor_self(n))
-            def _(src=src, dst=dst, m=m):
-                pltpu.make_async_copy(src, dst, f_recv.at[m]).start()
-
-            @pl.when(jnp.logical_not(factor_self(n)))
-            def _(src=src, dst=dst, m=m, n=n):
-                remote(src, dst, f_send.at[n, m], f_recv.at[m], device(z, x, owner, 2 * core + n)).start()
+        left_part(n)
+    lax.fori_loop(0, ROWS, send_left, 0)
+    for n in range(2):
+        right_part(n)
 
     for cp in x_copies:
         cp.wait()
     ar_y[y] = jnp.sum(ar_x[...], axis=0)
     y_copies = spread(ar_y, y, NY, y_send, y_recv, lambda o: device(z, x, core, o))
 
-    drain(rrb.at[:, pl.ds(core * half, half)], rr_recv)
+    drain(rrb.at[:, pl.ds(core * half, half)], root_recv.at[1])
     rr_swap = remote(
         rrb.at[:, pl.ds(core * half, half)], rrb.at[:, pl.ds(core * half, half)], rx_send, rx_recv, partner
     )
     rr_swap.start()
-    drain(rlb, rl_recv)
+    drain(rlb, root_recv.at[0])
     rl = rlb[...].reshape(half, WIDTH)
     for c in range(NY):
         hb[:, c * COLS:(c + 1) * COLS] = jnp.dot(
@@ -217,14 +253,23 @@
     own_dir = pltpu.make_async_copy(sb.at[y, zx], ubr.at[mine], u_recv)
     own_dir.start()
 
-    def send_dir(k, _):
+    def send_dir(k):
         tz, tx, ty = target(k)
         remote(
             sb.at[ty, tz * NX + tx], ubr.at[mine], u_send, u_recv, device(tz, tx, core, ty)
         ).start()
-        return 0
-
-    lax.fori_loop(1, SLOTS, send_dir, 0)
+
+    def send_back(n, _):
+        for u in range(8):
+            @pl.when(n * 8 + u > 0)
+            def _(u=u):
+                send_dir(n * 8 + u)
+
+            if u % 4 == 3:
+                send_factor(1, u // 4, n)
+        return 0
+
+    lax.fori_loop(0, ROWS, send_back, 0)
 
     drain(ubr, u_recv)
 
@@ -245,13 +290,13 @@
         for q in range(NC):
             @pl.when(jnp.logical_not(is_self(i, q)))
             def _(i=i, q=q):
-                for src, dst, send, recv in root_parts(i, q):
-                    drain(dst, send)
+                drain(rlb.at[pl.ds(0, 8)], root_send.at[0, i, q])
+                drain(rrb.at[0, pl.ds(0, half)], root_send.at[1, i, q])
     for n in range(2):
         @pl.when(jnp.logical_not(factor_self(n)))
         def _(n=n):
-            drain(lb.at[n], f_send.at[n, 0])
-            drain(rb.at[n], f_send.at[n, 1])
+            drain(lb.at[n], f_send.at[0, n])
+            drain(rb.at[n], f_send.at[1, n])
 
 
 def exchange(block_slot, inverse, gradients, adagrad, root_left, root_right):
@@ -263,12 +308,16 @@
         kernel,
         out_shape=(
             jax.ShapeDtypeStruct((NBLK, ROWS, COLS), BF16),
-            jax.ShapeDtypeStruct((2, COLS, WIDTH), BF16),
-            jax.ShapeDtypeStruct((2, COLS, WIDTH), BF16),
+            jax.ShapeDtypeStruct((2, ROWS, ROWS, WIDTH), BF16),
+            jax.ShapeDtypeStruct((2, ROWS, ROWS, WIDTH), BF16),
         ),
-        in_specs=[smem, smem, vmem, vmem, hbm, hbm],
+        in_specs=[smem, smem, hbm, hbm, hbm, hbm],
         out_specs=(vmem, hbm, hbm),
         scratch_shapes=[
+            pltpu.VMEM((NBLK, ROWS, COLS), BF16),
+            pltpu.VMEM((NBLK, ROWS, COLS), F32),
+            dma((2,)),
+            pltpu.SemaphoreType.REGULAR((2,)),
             pltpu.VMEM((SLOTS, ROWS, COLS), BF16),
             pltpu.VMEM((NY, NZ * NX, NC, ROWS, COLS), BF16),
             pltpu.VMEM((NZ * NX, ROWS, WIDTH), BF16),
@@ -276,19 +325,19 @@
             pltpu.VMEM((WIDTH // 2, WIDTH), BF16),
             pltpu.VMEM((NY, NZ * NX, ROWS, COLS), BF16),
             pltpu.VMEM((SLOTS, ROWS, COLS), BF16),
-            pltpu.VMEM((2, COLS, WIDTH), BF16),
-            pltpu.VMEM((2, COLS, WIDTH), BF16),
+            pltpu.VMEM((2, ROWS, ROWS, WIDTH), BF16),
+            pltpu.VMEM((2, ROWS, ROWS, WIDTH), BF16),
             pltpu.VMEM((128, 128), F32),
             pltpu.VMEM((NZ, 8, 128), F32),
             pltpu.VMEM((NX, 8, 128), F32),
             pltpu.VMEM((NY, 8, 128), F32),
             pltpu.VMEM((NC, 2, 8, 128), F32),
-            dma, dma((NY,)), dma((NY,)), dma((NY,)), dma((2, NC)), dma, dma((2, NC)), dma,
+            dma, dma((NY,)), dma((NY,)), dma((NY,)), dma((2, 2, NC)), dma((2,)),
             dma, dma, dma((2, 2)), dma((2,)), dma, dma,
             dma((NZ,)), dma((NZ,)), dma((NX,)), dma((NX,)), dma((NY,)), dma((NY,)), dma, dma,
         ],
         compiler_params=pltpu.CompilerParams(
-            collective_id=0, has_side_effects=True, vmem_limit_bytes=48 * 2**20
+            collective_id=0, has_side_effects=True, vmem_limit_bytes=56 * 2**20
         ),
         name="shampoo_exchange",
     )(block_slot, inverse, gradients, adagrad, root_left, root_right)
@@ -305,8 +354,8 @@
     )
     grads32 = gradients.astype(F32)
     adagrad_new = adagrad + grads32 * grads32
-    factor_left_new = 0.9 * factor_left + 0.1 * left_term.astype(F32)
-    factor_right_new = 0.9 * factor_right + 0.1 * right_term.astype(F32)
+    factor_left_new = 0.9 * factor_left + 0.1 * left_term.reshape(factor_left.shape).astype(F32)
+    factor_right_new = 0.9 * factor_right + 0.1 * right_term.reshape(factor_right.shape).astype(F32)
     return update, adagrad_new, factor_left_new, factor_right_new
 
 

time: 118 us -> 101 us (0.86)
  Pallas kernels: 103 us -> 89.2 us
  local copies, waits for them, and re-layouts: 6.07 us -> 1.01 us
  other arithmetic: 6.32 us -> 8.13 us
    pallas_call x1, Pallas kernels: 103 us -> 89.2 us  [exchange(): pl.pallas_call(kernel, out_shape=(jax.ShapeDtypeStruct((NBLK, ROWS, COLS)...]
    unnamed x13 -> x11, local copies, waits for them, and re-layouts: 6.07 us -> 1.01 us
    mul x0 -> x1, other arithmetic: none -> 2.29 us  [on_device(): 0.1 * right_term.reshape(factor_right.shape).astype(F32)]
    add x1 -> x2, other arithmetic: 4.5 us -> 3.52 us  [the longest x1 1.76 us: on_device(): 0.9 * factor_right]
where the time goes in v2:
time: 101 us; the launch traced here: 99 us
  Pallas kernels  89.2 us (88%)
  other arithmetic  8.13 us (8%)
  local copies, waits for them, and re-layouts  1.01 us (1%)
    pallas_call x1, Pallas kernels, exchange(): pl.pallas_call(kernel, out_shape=(jax.ShapeDtypeStruct((NBLK, ROWS, COLS)...  89.2 us
    mul x1, other arithmetic, on_device(): 0.1 * right_term.reshape(factor_right.shape).astype(F32)  2.29 us

profile of v2, /device:TPU:9, one launch (start us, length us, event | category | flops | bytes accessed | tf_op | source)
XLA Modules:
  0.0 99.0 jit_solution(11005773966189042135)
XLA Ops:
  0.6 1.3 %select_reduce_fusion.inv_ref = s32[128]{0:T(128)} fusion(s32[56]{0:T(128)} %slot_ref.1), kind=kLoop, calls=%fused_computation.5 | loop fusion | flops 21376 | bytes 736 | tf_op jit(solution)/shard_map/reduce_min | solution.py:350
  1.9 89.2 %shampoo_exchange.1 = (bf16[56,16,256]{2,1,0:T(8,128)(2,1)}, bf16[2,16,16,1024]{3,2,1,0:T(8,128)(2,1)}, bf16[2,16,16,1024]{3,2,1,0:T(8,128)(2,1)}) custom-call(s32[56]{0:T(128)} %slot_ref.1, s32[128]{0:T(128)} %select_reduce_fusion.inv_ref, bf16[56,16,256]{2,1,0:T(8,128)(2,1)} %g_hbm.1, f32[56,16,256]{2,1,0:T(8,128)} %a_hbm.1, ...), custom_call_target="tpu_custom_call" | custom-call | tf_op jit(solution)/shard_map/shampoo_exchange/pallas_call | solution.py:307
  91.1 0.0 copy-start.1
  91.1 2.3 %convert_multiply_fusion = (f32[2,16,16,1024]{3,2,1,0:T(8,128)S(1)}, f32[2,16,16,1024]{3,2,1,0:T(8,128)S(1)}) fusion(bf16[2,16,16,1024]{3,2,1,0:T(8,128)(2,1)} %get-tuple-element.9, bf16[2,16,16,1024]{3,2,1,0:T(8,128)(2,1)} %get-tuple-element.8), kind=kLoop, calls=%fused_computation.2 | loop fusion | flops 2097152 | bytes 6291456 | tf_op jit(solution)/shard_map/mul | solution.py:358
  93.4 0.0 copy-done.1
  93.4 0.0 copy-start.2
  93.4 1.8 %bitcast_add_fusion = f32[2,256,1024]{2,1,0:T(8,128)} fusion(f32[2,16,16,1024]{3,2,1,0:T(8,128)S(1)} %get-tuple-element.10, f32[2,256,1024]{2,1,0:T(8,128)S(1)} %copy-done.1), kind=kLoop, calls=%fused_computation | loop fusion | flops 1048576 | bytes 6291456 | tf_op jit(solution)/shard_map/add | solution.py:358
  95.2 0.2 copy-done.2
  95.4 0.0 copy-start
  95.4 0.0 copy-start.3
  95.4 1.8 %bitcast_add_fusion.1 = f32[2,256,1024]{2,1,0:T(8,128)} fusion(f32[2,16,16,1024]{3,2,1,0:T(8,128)S(1)} %get-tuple-element.11, f32[2,256,1024]{2,1,0:T(8,128)S(1)} %copy-done.2), kind=kLoop, calls=%fused_computation.1 | loop fusion | flops 1048576 | bytes 6291456 | tf_op jit(solution)/shard_map/add | solution.py:357
  97.2 0.0 copy-start.4
  97.2 0.0 copy-done
  97.2 0.0 copy-done.3
  97.2 1.1 %multiply_add_fusion = f32[56,16,256]{2,1,0:T(8,128)} fusion(f32[56,16,256]{2,1,0:T(8,128)S(1)} %copy-done, bf16[56,16,256]{2,1,0:T(8,128)(2,1)S(1)} %copy-done.3), kind=kLoop, calls=%fused_computation.4 | loop fusion | flops 688128 | bytes 2293760 | tf_op jit(solution)/shard_map/add | solution.py:356
  98.3 0.0 copy-done.4
  98.3 0.8 copy.12
Async XLA Ops:
  91.1 2.3 %copy-start.1 = (f32[2,256,1024]{2,1,0:T(8,128)S(1)}, f32[2,256,1024]{2,1,0:T(8,128)}, u32[]{:S(2)}) copy-start(f32[2,256,1024]{2,1,0:T(8,128)} %param.10) | copy-start | bytes 6291460
  93.4 2.0 %copy-start.2 = (f32[2,256,1024]{2,1,0:T(8,128)S(1)}, f32[2,256,1024]{2,1,0:T(8,128)}, u32[]{:S(2)}) copy-start(f32[2,256,1024]{2,1,0:T(8,128)} %param.9) | copy-start | bytes 6291460
  95.4 1.8 %copy-start = (f32[56,16,256]{2,1,0:T(8,128)S(1)}, f32[56,16,256]{2,1,0:T(8,128)}, u32[]{:S(2)}) copy-start(f32[56,16,256]{2,1,0:T(8,128)} %a_hbm.1) | copy-start | bytes 2752516
  95.4 1.8 %copy-start.3 = (bf16[56,16,256]{2,1,0:T(8,128)(2,1)S(1)}, bf16[56,16,256]{2,1,0:T(8,128)(2,1)}, u32[]{:S(2)}) copy-start(bf16[56,16,256]{2,1,0:T(8,128)(2,1)} %g_hbm.1) | copy-start | bytes 1376260
  97.2 1.1 %copy-start.4 = (bf16[56,16,256]{2,1,0:T(8,128)(2,1)S(1)}, bf16[56,16,256]{2,1,0:T(8,128)(2,1)}, u32[]{:S(2)}) copy-start(bf16[56,16,256]{2,1,0:T(8,128)(2,1)} %get-tuple-element.16) | copy-start | bytes 1376260

commit v3 on v2

--- a/solution.py
+++ b/solution.py
@@ -17,14 +17,18 @@
     return (z * (NX * NC) + x * NC + core, y)
 
 
+def in_hbm(value):
+    return pltpu.with_memory_space_constraint(value, pltpu.HBM)
+
+
 def drain(ref, sem):
     pltpu.make_async_copy(ref, ref, sem).wait()
 
 
 def kernel(
-    slot_ref, inv_ref, g_hbm, a_hbm, rl_ref, rr_ref,
-    upd_ref, left_ref, right_ref,
-    g_ref, a_ref, in_sem, meet, sbuf, gbuf, rlb, rrb, hb, sb, ubr, lb, rb, gp, ar_z, ar_x, ar_y, ar_c,
+    slot_row, g_hbm, a_hbm, rl_ref, rr_ref,
+    ubr, left_ref, right_ref,
+    g_ref, a_ref, in_sem, meet, inv_v, inv_ref, sbuf, gbuf, rlb, rrb, hb, sb, lb, rb, gp, ar_z, ar_x, ar_y, ar_c,
     g_send, g_recv, gx_send, gx_recv, root_send, root_recv,
     rx_send, rx_recv, f_send, f_recv, u_send, u_recv,
     z_send, z_recv, x_send, x_recv, y_send, y_recv, c_send, c_recv,
@@ -66,9 +70,17 @@
     first = along_z + along_x + along_y + [partner]
     greet(barrier, first)
 
+    at_slot = lax.broadcasted_iota(jnp.int32, (SLOTS, NBLK), 0) == slot_row[...]
+    block = lax.broadcasted_iota(jnp.int32, (SLOTS, NBLK), 1)
+    block = jnp.min(jnp.where(at_slot, block, NBLK), axis=1, keepdims=True)
+    inv_v[...] = jnp.transpose(jnp.broadcast_to(block, (SLOTS, 128)))[:8]
+    to_smem = pltpu.make_async_copy(inv_v, inv_ref, in_sem.at[2])
+    to_smem.start()
+    to_smem.wait()
+
     def pack(t, _):
-        b = inv_ref[t]
-        rows = g_ref[jnp.minimum(b, NBLK - 1)]
+        b = inv_ref[0, t]
+        rows = g_ref[jnp.clip(b, 0, NBLK - 1)]
         sbuf[t] = jnp.where(b < NBLK, rows, jnp.zeros_like(rows))
         return 0
 
@@ -109,17 +121,20 @@
         def _():
             remote(src, dst, root_send.at[m, i, q], root_recv.at[m], device(z, x, q, 2 * core + i)).start()
 
-    def send_all(n, _):
-        for u, (i, q, m) in enumerate([(i, q, m) for i in range(2) for q in range(NC) for m in range(2)]):
-            @pl.when(n * 16 + 2 * u > 0)
+    def send_first(n, _):
+        for u in range(16):
+            @pl.when(n * 16 + u > 0)
             def _(u=u):
-                send_rows(n * 16 + 2 * u)
-
+                send_rows(n * 16 + u)
+        return 0
+
+    def send_roots(n, _):
+        for i, q, m in [(i, q, m) for i in range(2) for q in range(NC) for m in range(2)]:
             send_root(i, q, m, n)
-            send_rows(n * 16 + 2 * u + 1)
-        return 0
-
-    lax.fori_loop(0, 8, send_all, 0)
+        return 0
+
+    lax.fori_loop(0, 8, send_first, 0)
+    lax.fori_loop(0, 1, send_roots, 0)
 
     gp[...] = jnp.zeros_like(gp)
 
@@ -133,7 +148,7 @@
     loads[1].wait()
     lax.fori_loop(0, NBLK, graft, 0)
     part = jnp.sum(jnp.transpose(gp[...]), axis=0, keepdims=True)
-    ar_z[z] = jnp.broadcast_to(part, (8, 128))
+    ar_y[y] = jnp.broadcast_to(part, (8, 128))
 
     def spread(buf, me, count, send, recv, where):
         copies = []
@@ -144,6 +159,15 @@
             cp.start()
         return copies
 
+    y_copies = spread(ar_y, y, NY, y_send, y_recv, lambda o: device(z, x, core, o))
+    lax.fori_loop(1, 8, send_roots, 0)
+    for cp in y_copies:
+        cp.wait()
+    ar_x[x] = jnp.sum(ar_y[...], axis=0)
+    x_copies = spread(ar_x, x, NX, x_send, x_recv, lambda o: device(z, o, core, y))
+    for cp in x_copies:
+        cp.wait()
+    ar_z[z] = jnp.sum(ar_x[...], axis=0)
     z_copies = spread(ar_z, z, NZ, z_send, z_recv, lambda o: device(o, x, core, y))
 
     swaps = []
@@ -152,10 +176,6 @@
         cp = remote(gbuf.at[c, :, core], gbuf.at[c, :, core], gx_send.at[c], gx_recv.at[c], partner)
         cp.start()
         swaps.append(cp)
-    for cp in z_copies:
-        cp.wait()
-    ar_x[x] = jnp.sum(ar_z[...], axis=0)
-    x_copies = spread(ar_x, x, NX, x_send, x_recv, lambda o: device(z, o, core, y))
     for cp in swaps:
         cp.wait_recv()
 
@@ -170,21 +190,22 @@
             acc = acc + lax.dot_general(
                 rows, gbuf[c].reshape(WIDTH, COLS), (((1,), (1,)), ((), ())), preferred_element_type=F32
             )
-        lb[n] = acc.astype(BF16).reshape(ROWS, ROWS, WIDTH)
+        lb[n] = acc.astype(BF16)
 
     def right_part(n):
         cols = gbuf[2 * core + n].reshape(WIDTH, COLS)
         for c in range(NY):
-            rb[n, :, :, c * COLS:(c + 1) * COLS] = lax.dot_general(
+            rb[n, :, c * COLS:(c + 1) * COLS] = lax.dot_general(
                 cols, gbuf[c].reshape(WIDTH, COLS), (((0,), (0,)), ((), ())), preferred_element_type=F32
-            ).astype(BF16).reshape(ROWS, ROWS, COLS)
+            ).astype(BF16)
 
     def factor_self(n):
         return jnp.logical_and(2 * core + n == y, core == owner)
 
     def send_factor(m, n, piece):
-        src = (lb, rb)[m].at[n, piece]
-        dst = (left_ref, right_ref)[m].at[i_mine, piece]
+        rows = pl.ds(pl.multiple_of(piece * ROWS, ROWS), ROWS)
+        src = (lb, rb)[m].at[n, rows]
+        dst = (left_ref, right_ref)[m].at[i_mine, rows]
 
         @pl.when(factor_self(n))
         def _():
@@ -204,11 +225,6 @@
     lax.fori_loop(0, ROWS, send_left, 0)
     for n in range(2):
         right_part(n)
-
-    for cp in x_copies:
-        cp.wait()
-    ar_y[y] = jnp.sum(ar_x[...], axis=0)
-    y_copies = spread(ar_y, y, NY, y_send, y_recv, lambda o: device(z, x, core, o))
 
     drain(rrb.at[:, pl.ds(core * half, half)], root_recv.at[1])
     rr_swap = remote(
@@ -229,55 +245,54 @@
         s32 = s.astype(F32)
         s2 = jnp.sum((s32 * s32).reshape(half // 8, 8, COLS), axis=0)
         sq = sq + s2[:, :128] + s2[:, 128:]
-    for cp in y_copies:
+    for cp in z_copies:
         cp.wait()
     ar_c[core, 0] = sq
-    ar_c[core, 1] = jnp.sum(ar_y[...], axis=0)
+    ar_c[core, 1] = jnp.sum(ar_z[...], axis=0)
     c_copy = remote(ar_c.at[core], ar_c.at[core], c_send, c_recv, partner)
     c_copy.start()
     c_copy.wait()
     search_sq = jnp.sum(ar_c[0, 0] + ar_c[1, 0], keepdims=True)
     graft_all = ar_c[0, 1, 0:1] + ar_c[1, 1, 0:1]
     lane = lax.broadcasted_iota(jnp.int32, (1, 128), 1)
-    graft_sq = jnp.sum(jnp.where(lane == inv_ref[mine], graft_all, 0.0), keepdims=True)
+    graft_sq = jnp.sum(jnp.where(lane == inv_ref[0, mine], graft_all, 0.0), keepdims=True)
     ratio = jnp.sqrt(graft_sq) / (jnp.sqrt(search_sq) + 1e-06)
     ratio = jnp.broadcast_to(ratio, (1, COLS))
 
     def scale(k, _):
+        few = pl.ds(k * 4, 4)
         for c in range(NY):
-            sb[c, k] = (sb[c, k].astype(F32) * ratio).astype(BF16)
-        return 0
-
-    lax.fori_loop(0, NZ * NX, scale, 0)
+            sb[c, few] = (sb[c, few].astype(F32) * ratio).astype(BF16)
+        return 0
+
+    lax.fori_loop(0, NZ * NX // 4, scale, 0)
 
     own_dir = pltpu.make_async_copy(sb.at[y, zx], ubr.at[mine], u_recv)
     own_dir.start()
 
     def send_dir(k):
-        tz, tx, ty = target(k)
+        m = k % (NZ * NX) * 13
+        tz, tx, ty = (z + m % NZ) % NZ, (x + (m // NZ) % NX) % NX, (y + k // (NZ * NX)) % NY
         remote(
             sb.at[ty, tz * NX + tx], ubr.at[mine], u_send, u_recv, device(tz, tx, core, ty)
         ).start()
 
     def send_back(n, _):
-        for u in range(8):
-            @pl.when(n * 8 + u > 0)
+        for u in range(16):
+            @pl.when(n * 16 + u > 0)
             def _(u=u):
-                send_dir(n * 8 + u)
-
-            if u % 4 == 3:
-                send_factor(1, u // 4, n)
-        return 0
-
-    lax.fori_loop(0, ROWS, send_back, 0)
+                send_dir(n * 16 + u)
+        return 0
+
+    def send_right(piece, _):
+        for n in range(2):
+            send_factor(1, n, piece)
+        return 0
+
+    lax.fori_loop(0, 8, send_back, 0)
+    lax.fori_loop(0, ROWS, send_right, 0)
 
     drain(ubr, u_recv)
-
-    def pick(b, _):
-        upd_ref[b] = ubr[slot_ref[b]]
-        return 0
-
-    lax.fori_loop(0, NBLK, pick, 0)
 
     drain(left_ref, f_recv.at[0])
     drain(right_ref, f_recv.at[1])
@@ -299,34 +314,34 @@
             drain(rb.at[n], f_send.at[1, n])
 
 
-def exchange(block_slot, inverse, gradients, adagrad, root_left, root_right):
+def exchange(block_slot, gradients, adagrad, root_left, root_right):
     vmem = pl.BlockSpec(memory_space=pltpu.VMEM)
-    smem = pl.BlockSpec(memory_space=pltpu.SMEM)
     hbm = pl.BlockSpec(memory_space=pl.ANY)
     dma = pltpu.SemaphoreType.DMA
     return pl.pallas_call(
         kernel,
         out_shape=(
-            jax.ShapeDtypeStruct((NBLK, ROWS, COLS), BF16),
-            jax.ShapeDtypeStruct((2, ROWS, ROWS, WIDTH), BF16),
-            jax.ShapeDtypeStruct((2, ROWS, ROWS, WIDTH), BF16),
+            pltpu.VMEM((SLOTS, ROWS, COLS), BF16),
+            pltpu.VMEM((2, COLS, WIDTH), BF16),
+            pltpu.VMEM((2, COLS, WIDTH), BF16),
         ),
-        in_specs=[smem, smem, hbm, hbm, hbm, hbm],
-        out_specs=(vmem, hbm, hbm),
+        in_specs=[vmem, hbm, hbm, hbm, hbm],
+        out_specs=(hbm, hbm, hbm),
         scratch_shapes=[
             pltpu.VMEM((NBLK, ROWS, COLS), BF16),
             pltpu.VMEM((NBLK, ROWS, COLS), F32),
-            dma((2,)),
+            dma((3,)),
             pltpu.SemaphoreType.REGULAR((2,)),
+            pltpu.VMEM((8, 128), jnp.int32),
+            pltpu.SMEM((8, 128), jnp.int32),
             pltpu.VMEM((SLOTS, ROWS, COLS), BF16),
             pltpu.VMEM((NY, NZ * NX, NC, ROWS, COLS), BF16),
             pltpu.VMEM((NZ * NX, ROWS, WIDTH), BF16),
             pltpu.VMEM((NY, WIDTH, COLS), BF16),
             pltpu.VMEM((WIDTH // 2, WIDTH), BF16),
             pltpu.VMEM((NY, NZ * NX, ROWS, COLS), BF16),
-            pltpu.VMEM((SLOTS, ROWS, COLS), BF16),
-            pltpu.VMEM((2, ROWS, ROWS, WIDTH), BF16),
-            pltpu.VMEM((2, ROWS, ROWS, WIDTH), BF16),
+            pltpu.VMEM((2, COLS, WIDTH), BF16),
+            pltpu.VMEM((2, COLS, WIDTH), BF16),
             pltpu.VMEM((128, 128), F32),
             pltpu.VMEM((NZ, 8, 128), F32),
             pltpu.VMEM((NX, 8, 128), F32),
@@ -337,25 +352,96 @@
             dma((NZ,)), dma((NZ,)), dma((NX,)), dma((NX,)), dma((NY,)), dma((NY,)), dma, dma,
         ],
         compiler_params=pltpu.CompilerParams(
-            collective_id=0, has_side_effects=True, vmem_limit_bytes=56 * 2**20
+            collective_id=0, has_side_effects=True, vmem_limit_bytes=24 * 2**20
         ),
+        cost_estimate=pl.CostEstimate(flops=6 * 10**10, bytes_accessed=6 * 2**20, transcendentals=0),
         name="shampoo_exchange",
-    )(block_slot, inverse, gradients, adagrad, root_left, root_right)
+    )(block_slot.reshape(1, NBLK), *(in_hbm(v) for v in (gradients, adagrad, root_left, root_right)))
+
+
+def tail_kernel(
+    slot, fl, fr, left, right, g, a, directions, fl_out, fr_out, a_out, upd_out,
+    f_buf, t_buf, g_buf, a_buf, f_in, t_in, ga_in, f_sem, a_sem, u_sem,
+):
+    parts = 4
+    rows = 2 * COLS // parts
+    ins, outs = [], []
+    terms = [pltpu.make_async_copy(src, t_buf.at[m], t_in.at[m]) for m, src in enumerate((left, right))]
+    for m, (src, out) in enumerate(((fl, fl_out), (fr, fr_out))):
+        for n in range(parts):
+            i, r0 = n * rows // COLS, n * rows % COLS
+            cut = (i, pl.ds(r0, rows))
+            ins.append((m, cut, out, pltpu.make_async_copy(src.at[cut], f_buf.at[(m,) + cut], f_in.at[m, n])))
+            ins[-1][-1].start()
+        terms[m].start()
+    g_copy = pltpu.make_async_copy(g, g_buf, ga_in.at[0])
+    a_copy = pltpu.make_async_copy(a, a_buf, ga_in.at[1])
+    g_copy.start()
+    a_copy.start()
+
+    def place(b, _):
+        pltpu.make_async_copy(directions.at[slot[b]], upd_out.at[b], u_sem).start()
+        return 0
+
+    lax.fori_loop(0, NBLK, place, 0)
+    for n, (m, cut, out, copy) in enumerate(ins):
+        copy.wait()
+        if n % parts == 0:
+            terms[m].wait()
+        f_buf[(m,) + cut] = 0.9 * f_buf[(m,) + cut] + 0.1 * t_buf[(m,) + cut].astype(F32)
+        outs.append(pltpu.make_async_copy(f_buf.at[(m,) + cut], out.at[cut], f_sem.at[m, n % parts]))
+        outs[-1].start()
+    g_copy.wait()
+    a_copy.wait()
+
+    def add(n, _):
+        few = pl.ds(n * 4, 4)
+        g32 = g_buf[few].astype(F32)
+        a_buf[few] = a_buf[few] + g32 * g32
+        return 0
+
+    lax.fori_loop(0, NBLK // 4, add, 0)
+    outs.append(pltpu.make_async_copy(a_buf, a_out, a_sem))
+    outs[-1].start()
+    for copy in outs:
+        copy.wait()
+    drain(upd_out, u_sem)
+
+
+def tail(block_slot, factor_left, factor_right, left_term, right_term, gradients, adagrad, directions):
+    smem = pl.BlockSpec(memory_space=pltpu.SMEM)
+    hbm = pl.BlockSpec(memory_space=pl.ANY)
+    dma = pltpu.SemaphoreType.DMA
+    return pl.pallas_call(
+        tail_kernel,
+        out_shape=(
+            jax.ShapeDtypeStruct(factor_left.shape, F32),
+            jax.ShapeDtypeStruct(factor_right.shape, F32),
+            jax.ShapeDtypeStruct(adagrad.shape, F32),
+            jax.ShapeDtypeStruct(gradients.shape, BF16),
+        ),
+        in_specs=[smem] + [hbm] * 7,
+        out_specs=(hbm, hbm, hbm, hbm),
+        scratch_shapes=[
+            pltpu.VMEM((2, 2, COLS, WIDTH), F32),
+            pltpu.VMEM((2, 2, COLS, WIDTH), BF16),
+            pltpu.VMEM((NBLK, ROWS, COLS), BF16),
+            pltpu.VMEM((NBLK, ROWS, COLS), F32),
+            dma((2, 4)), dma((2,)), dma((2,)), dma((2, 4)), dma, dma,
+        ],
+        compiler_params=pltpu.CompilerParams(vmem_limit_bytes=16 * 2**20),
+        name="shampoo_tail",
+    )(block_slot, factor_left, factor_right, left_term, right_term, gradients, adagrad, directions)
 
 
 def on_device(gradients, adagrad, factor_left, factor_right, root_left, root_right, block_slot):
     count = factor_left.shape[0]
-    numbers = jnp.arange(NBLK, dtype=jnp.int32)
-    named = jnp.arange(SLOTS, dtype=jnp.int32)[:, None] == block_slot[None, :]
-    inverse = jnp.min(jnp.where(named, numbers[None, :], NBLK), axis=1)
-    update, left_term, right_term = exchange(
-        block_slot, inverse, gradients, adagrad,
-        root_left.reshape(count, 8, NC, ROWS, WIDTH), root_right,
+    directions, left_term, right_term = exchange(
+        block_slot, gradients, adagrad, root_left.reshape(count, 8, NC, ROWS, WIDTH), root_right
     )
-    grads32 = gradients.astype(F32)
-    adagrad_new = adagrad + grads32 * grads32
-    factor_left_new = 0.9 * factor_left + 0.1 * left_term.reshape(factor_left.shape).astype(F32)
-    factor_right_new = 0.9 * factor_right + 0.1 * right_term.reshape(factor_right.shape).astype(F32)
+    factor_left_new, factor_right_new, adagrad_new, update = tail(
+        block_slot, factor_left, factor_right, left_term, right_term, gradients, adagrad, directions
+    )
     return update, adagrad_new, factor_left_new, factor_right_new
 
 

time: 101 us -> 91.5 us (0.906)
  other arithmetic: 8.13 us -> 0 us
    add x3 -> x0, other arithmetic: 4.59 us -> none  [the longest x1 1.76 us: on_device(): 0.9 * factor_right]
    mul x1 -> x0, other arithmetic: 2.29 us -> none  [on_device(): 0.1 * right_term.reshape(factor_right.shape).astype(F32)]
    reduce_min x1 -> x0, other arithmetic: 1.26 us -> none  [on_device(): inverse = jnp.min(jnp.where(named, numbers[None, :], NBLK), axis=1)]
    pallas_call x1 -> x2, Pallas kernels: 89.2 us -> 88.4 us  [the longest x1 84.1 us: exchange(): pl.pallas_call(kernel, out_shape=(pltpu.VMEM((SLOTS, ROWS, COLS), BF16),...]
where the time goes in v3:
time: 91.5 us; the launch traced here: 89.8 us
  Pallas kernels  88.4 us (97%)
    pallas_call x1, Pallas kernels, exchange(): pl.pallas_call(kernel, out_shape=(pltpu.VMEM((SLOTS, ROWS, COLS), BF16),...  84.1 us
    pallas_call x1, Pallas kernels, tail(): pl.pallas_call(tail_kernel, out_shape=(jax.ShapeDtypeStruct(factor_left.s...  4.36 us

profile of v3, /device:TPU:9, one launch (start us, length us, event | category | flops | bytes accessed | tf_op | source)
XLA Modules:
  0.0 89.8 jit_solution(272352879511871307)
XLA Ops:
  0.6 0.0 copy-start.4
  0.6 0.6 copy-done.4
  1.3 0.0 copy-start
  1.3 0.0 copy-start.1
  1.3 0.0 copy-start.2
  1.3 0.0 copy-start.3
  1.3 84.1 %shampoo_exchange.1 = (bf16[128,16,256]{2,1,0:T(8,128)(2,1)S(1)}, bf16[2,256,1024]{2,1,0:T(8,128)(2,1)S(1)}, bf16[2,256,1024]{2,1,0:T(8,128)(2,1)S(1)}) custom-call(s32[1,56]{1,0:T(1,128)S(1)} %bitcast.2, bf16[56,16,256]{2,1,0:T(8,128)(2,1)} %g.1, f32[56,16,256]{2,1,0:T(8,128)} %a.1, bf16[2,8,2,16,1024]{4,3,2,1,0:T(8,128)(2,1)} %bitcast.3, ...), custom_call_target="tpu_custom_call" | custom-call | flops 60000002048 | bytes 6291456 | tf_op jit(solution)/shard_map/shampoo_exchange/pallas_call | solution.py:321
  85.4 0.0 copy-done
  85.4 0.0 copy-done.1
  85.4 0.0 copy-done.2
  85.4 0.0 copy-done.3
  85.4 4.4 %shampoo_tail.1 = (f32[2,256,1024]{2,1,0:T(8,128)}, f32[2,256,1024]{2,1,0:T(8,128)}, f32[56,16,256]{2,1,0:T(8,128)}, bf16[56,16,256]{2,1,0:T(8,128)(2,1)}) custom-call(s32[56]{0:T(128)S(1)} %copy-done.4, f32[2,256,1024]{2,1,0:T(8,128)S(1)} %copy-done, f32[2,256,1024]{2,1,0:T(8,128)S(1)} %copy-done.1, bf16[2,256,1024]{2,1,0:T(8,128)(2,1)S(1)} %get-tuple-element.11.left, ...), custom_call_target="tpu_custom_call" | custom-call | tf_op jit(solution)/shard_map/shampoo_tail/pallas_call | solution.py:415
Async XLA Ops:
  0.6 0.7 copy-start.4
  1.3 84.1 %copy-start = (f32[2,256,1024]{2,1,0:T(8,128)S(1)}, f32[2,256,1024]{2,1,0:T(8,128)}, u32[]{:S(2)}) copy-start(f32[2,256,1024]{2,1,0:T(8,128)} %fl.1) | copy-start | bytes 6291460
  1.3 84.1 %copy-start.1 = (f32[2,256,1024]{2,1,0:T(8,128)S(1)}, f32[2,256,1024]{2,1,0:T(8,128)}, u32[]{:S(2)}) copy-start(f32[2,256,1024]{2,1,0:T(8,128)} %fr.1) | copy-start | bytes 6291460
  1.3 84.1 %copy-start.2 = (f32[56,16,256]{2,1,0:T(8,128)S(1)}, f32[56,16,256]{2,1,0:T(8,128)}, u32[]{:S(2)}) copy-start(f32[56,16,256]{2,1,0:T(8,128)} %a.1) | copy-start | bytes 2752516
  1.3 84.1 %copy-start.3 = (bf16[56,16,256]{2,1,0:T(8,128)(2,1)S(1)}, bf16[56,16,256]{2,1,0:T(8,128)(2,1)}, u32[]{:S(2)}) copy-start(bf16[56,16,256]{2,1,0:T(8,128)(2,1)} %g.1) | copy-start | bytes 1376260

commit v4 on v3

v4 whole, which is shorter than its diff:
```python
import jax
import jax.numpy as jnp
from jax import lax
from jax.experimental import pallas as pl
from jax.experimental.pallas import tpu as pltpu
from jax.sharding import PartitionSpec as P

MESH = pl.DeviceIdType.MESH
NZ, NX, NC, NY = 8, 4, 2, 4
ROWS, COLS, WIDTH = 16, 256, 1024
SLOTS = NZ * NX * NY
NBLK = 56
F32, BF16 = jnp.float32, jnp.bfloat16


def device(z, x, core, y):
    return (z * (NX * NC) + x * NC + core, y)


def in_hbm(value):
    return pltpu.with_memory_space_constraint(value, pltpu.HBM)


def drain(ref, sem):
    pltpu.make_async_copy(ref, ref, sem).wait()


def kernel(
    slot_hbm, g_hbm, a_hbm, rl_ref, rr_ref,
    ubr, left_ref, right_ref, ratio_ref,
    g_ref, a_ref, in_sem, meet, slot_row, inv_v, inv_ref, sbuf, gbuf, rlb, rrb, hb, sb, lb, rb, gp, ar_z, ar_x, ar_y, ar_c, rt_z, rt_x, rt_y,
    g_send, g_recv, gx_send, gx_recv, root_send, rl_recv, rr_recv,
    rx_send, rx_recv, f_send, f_recv, u_send, u_recv,
    z_send, z_recv, x_send, x_recv, y_send, y_recv, c_send, c_recv,
):
    d = lax.axis_index("dp")
    y = lax.axis_index("replica")
    z, x, core = d // (NX * NC), (d // NC) % NX, d % NC
    other = 1 - core
    zx = z * NX + x
    mine = zx * NY + y
    partner = device(z, x, other, y)

    def target(k):
        m = (k * 37) % SLOTS
        return (z + m % NZ) % NZ, (x + (m // NZ) % NX) % NX, (y + m // (NZ * NX)) % NY

    def remote(src, dst, send, recv, where):
        return pltpu.make_async_remote_copy(
            src_ref=src, dst_ref=dst, send_sem=send, recv_sem=recv,
            device_id=where, device_id_type=MESH,
        )

    loads = [
        pltpu.make_async_copy(g_hbm, g_ref, in_sem.at[0]),
        pltpu.make_async_copy(a_hbm, a_ref, in_sem.at[1]),
        pltpu.make_async_copy(slot_hbm, slot_row, in_sem.at[3]),
    ]
    for cp in loads[::-1]:
        cp.start()

    along_z = [device((z + k) % NZ, x, core, y) for k in range(1, NZ)]
    along_x = [device(z, (x + k) % NX, core, y) for k in range(1, NX)]
    along_y = [device(z, x, core, (y + k) % NY) for k in range(1, NY)]
    barrier = pltpu.get_barrier_semaphore()

    def greet(sem, devices):
        for one in devices:
            pl.semaphore_signal(sem, inc=1, device_id=one, device_id_type=MESH)

    first = along_z + along_x + along_y + [partner]
    greet(barrier, first)

    loads[2].wait()
    at_slot = lax.broadcasted_iota(jnp.int32, (SLOTS, NBLK), 0) == slot_row[...]
    block = lax.broadcasted_iota(jnp.int32, (SLOTS, NBLK), 1)
    block = jnp.min(jnp.where(at_slot, block, NBLK), axis=1, keepdims=True)
    inv_v[...] = jnp.transpose(jnp.broadcast_to(block, (SLOTS, 128)))[:8]
    to_smem = pltpu.make_async_copy(inv_v, inv_ref, in_sem.at[2])
    to_smem.start()

    pl.semaphore_wait(barrier, len(first))
    greet(meet.at[0], along_y)
    to_smem.wait()
    loads[0].wait()
    pl.semaphore_wait(meet.at[0], len(along_y))
    greet(meet.at[1], along_x)

    half = WIDTH // 2

    def pack(t):
        b = inv_ref[0, t]
        rows = g_ref[jnp.clip(b, 0, NBLK - 1)]
        sbuf[t] = jnp.where(b < NBLK, rows, jnp.zeros_like(rows))

    def send_rows(k):
        tz, tx, ty = target(k)
        t = (tz * NX + tx) * NY + ty
        pack(t)
        remote(
            sbuf.at[t], gbuf.at[y, zx, core], g_send, g_recv.at[y], device(tz, tx, core, ty)
        ).start()

    def is_self(i, q):
        return jnp.logical_and(2 * core + i == y, core == q)

    def send_root(i, q, m, n):
        if m == 0:
            src, dst, recv = rl_ref.at[i, n, q], rlb.at[y * 8 + n], rl_recv
        else:
            rows = pl.ds(pl.multiple_of(q * half + n * (half // 8), half // 8), half // 8)
            src, dst, recv = rr_ref.at[i, rows], rrb.at[y, rows], rr_recv.at[y]

        @pl.when(is_self(i, q))
        def _():
            pltpu.make_async_copy(src, dst, recv).start()

        @pl.when(jnp.logical_not(is_self(i, q)))
        def _():
            remote(src, dst, root_send.at[m, i, q], recv, device(z, x, q, 2 * core + i)).start()

    def first_roots(n, _):
        for i, q in [(i, q) for i in range(2) for q in range(NC)]:
            send_root(i, q, 0, n)
        return 0

    lax.fori_loop(0, 2, first_roots, 0)
    pack(mine)
    own_rows = pltpu.make_async_copy(sbuf.at[mine], gbuf.at[y, zx, core], g_recv.at[y])
    own_rows.start()
    pl.semaphore_wait(meet.at[1], len(along_x))

    def send_some(m, first):
        def some(n, _):
            for u in range(16):
                k = (first + n) * 16 + u

                @pl.when(k > 0)
                def _(k=k):
                    send_rows(k)

                if u % 2 == 1:
                    piece = u // 2

                    @pl.when(k >= 16)
                    def _(piece=piece, n=n):
                        send_root(piece // 2 % 2, piece % 2, m, 2 * n + piece // 4)
            return 0

        return some

    lax.fori_loop(0, 4, send_some(0, 0), 0)
    lax.fori_loop(0, 4, send_some(1, 4), 0)

    gp[...] = jnp.zeros_like(gp)

    def graft(b, _):
        g32 = g_ref[b].astype(F32)
        scaled = g32 / (jnp.sqrt(a_ref[b] + g32 * g32) + 1e-08)
        sq = jnp.sum(scaled * scaled, axis=0, keepdims=True)
        gp[pl.ds(b, 1), :] = sq[:, :128] + sq[:, 128:]
        return 0

    loads[1].wait()
    lax.fori_loop(0, NBLK, graft, 0)
    part = jnp.sum(jnp.transpose(gp[...]), axis=0, keepdims=True)
    def spread(buf, me, count, send, recv, where):
        copies = []
        for k in range(1, count):
            other_one = (me + k) % count
            copies.append(remote(buf.at[me], buf.at[me], send.at[k], recv.at[k], where(other_one)))
        for cp in copies:
            cp.start()
        return copies

    def along(axis, buf, value, count, send, recv):
        me = (z, x, y)[axis]
        buf[me] = value
        return spread(buf, me, count, send, recv, lambda o: device(
            o if axis == 0 else z, o if axis == 1 else x, core, o if axis == 2 else y))

    def finish(copies, buf):
        for cp in copies:
            cp.wait()
        return jnp.sum(buf[...], axis=0)

    x_copies = along(1, ar_x, jnp.broadcast_to(part, (8, 128)), NX, x_send.at[0], x_recv.at[0])
    graft_x = finish(x_copies, ar_x)
    z_copies = along(0, ar_z, graft_x, NZ, z_send.at[0], z_recv.at[0])

    swaps = []
    for c in range(NY):
        drain(gbuf.at[c, :, core], g_recv.at[c])
        cp = remote(gbuf.at[c, :, core], gbuf.at[c, :, core], gx_send.at[c], gx_recv.at[c], partner)
        cp.start()
        swaps.append(cp)
    y_copies = along(2, ar_y, finish(z_copies, ar_z), NY, y_send.at[0], y_recv.at[0])
    for cp in swaps:
        cp.wait_recv()

    owner = y // 2
    i_mine = y % 2

    def left_part(n):
        r = 2 * core + n
        acc = jnp.zeros((COLS, WIDTH), F32)
        for c in range(NY):
            rows = gbuf[c, pl.ds(r * 8, 8)].reshape(COLS, COLS)
            acc = acc + lax.dot_general(
                rows, gbuf[c].reshape(WIDTH, COLS), (((1,), (1,)), ((), ())), preferred_element_type=F32
            )
        lb[n] = acc.astype(BF16)

    def right_part(n):
        cols = gbuf[2 * core + n].reshape(WIDTH, COLS)
        for c in range(NY):
            rb[n, :, c * COLS:(c + 1) * COLS] = lax.dot_general(
                cols, gbuf[c].reshape(WIDTH, COLS), (((0,), (0,)), ((), ())), preferred_element_type=F32
            ).astype(BF16)

    def factor_self(n):
        return jnp.logical_and(2 * core + n == y, core == owner)

    def send_factor(m, n, piece):
        rows = pl.ds(pl.multiple_of(piece * ROWS, ROWS), ROWS)
        src = (lb, rb)[m].at[n, rows]
        dst = (left_ref, right_ref)[m].at[i_mine, rows]

        @pl.when(factor_self(n))
        def _():
            pltpu.make_async_copy(src, dst, f_recv.at[m]).start()

        @pl.when(jnp.logical_not(factor_self(n)))
        def _():
            remote(src, dst, f_send.at[m, n], f_recv.at[m], device(z, x, owner, 2 * core + n)).start()

    def send_left(piece, _):
        for n in range(2):
            send_factor(0, n, piece)
        return 0

    for n in range(2):
        left_part(n)
    lax.fori_loop(0, ROWS, send_left, 0)
    for n in range(2):
        right_part(n)

    drain(rlb, rl_recv)
    rl = rlb[...].reshape(half, WIDTH)
    for c in range(NY):
        hb[:, c * COLS:(c + 1) * COLS] = jnp.dot(
            rl, gbuf[c].reshape(WIDTH, COLS), preferred_element_type=F32
        ).astype(BF16)

    def swap_root(c):
        part = rrb.at[c, pl.ds(pl.multiple_of(core * half, half), half)]
        drain(part, rr_recv.at[c])
        cp = remote(part, part, rx_send.at[c], rx_recv.at[c], partner)
        cp.start()
        return cp

    def send_back(c):
        def one(k, _):
            m = k * 13
            tz, tx = (z + m % NZ) % NZ, (x + (m // NZ) % NX) % NX
            remote(
                sb.at[c, tz * NX + tx], ubr.at[mine], u_send, u_recv, device(tz, tx, core, c)
            ).start()
            return 0

        return one

    sq = jnp.zeros((8, 128), F32)
    quarters = [(y + k) % NY for k in (0, 1, 3, 2)]
    root_swaps = [swap_root(quarters[0])]
    for k, c in enumerate(quarters):
        if k + 1 < NY:
            root_swaps.append(swap_root(quarters[k + 1]))
        root_swaps[k].wait_recv()
        s = jnp.dot(hb[...], rrb[c], preferred_element_type=F32).astype(BF16)
        sb[c] = s.reshape(NZ * NX, ROWS, COLS)
        if k == 0:
            own_dir = pltpu.make_async_copy(sb.at[y, zx], ubr.at[mine], u_recv)
            own_dir.start()
        lax.fori_loop(1 if k == 0 else 0, NZ * NX, send_back(c), 0)
        s32 = s.astype(F32)
        s2 = jnp.sum((s32 * s32).reshape(half // 8, 8, COLS), axis=0)
        sq = sq + s2[:, :128] + s2[:, 128:]

    ar_c[core, 0] = sq
    ar_c[core, 1] = finish(y_copies, ar_y)
    c_copy = remote(ar_c.at[core], ar_c.at[core], c_send, c_recv, partner)
    c_copy.start()
    c_copy.wait()
    search_sq = jnp.sum(ar_c[0, 0] + ar_c[1, 0], keepdims=True)
    graft_all = ar_c[0, 1] + ar_c[1, 1]
    lane = lax.broadcasted_iota(jnp.int32, (8, 128), 1)
    graft_sq = jnp.sum(jnp.where(lane[:1] == inv_ref[0, mine], graft_all[:1], 0.0), keepdims=True)
    ratio = jnp.sqrt(graft_sq) / (jnp.sqrt(search_sq) + 1e-06)
    ratio = jnp.where(lane == mine, jnp.broadcast_to(ratio, (8, 128)), 0.0)
    x_ratio = finish(along(1, rt_x, ratio, NX, x_send.at[1], x_recv.at[1]), rt_x)
    y_ratio = along(2, rt_y, x_ratio, NY, y_send.at[1], y_recv.at[1])

    def send_right(piece, _):
        for n in range(2):
            send_factor(1, n, piece)
        return 0

    lax.fori_loop(0, ROWS, send_right, 0)
    z_ratio = along(0, rt_z, finish(y_ratio, rt_y), NZ, z_send.at[1], z_recv.at[1])
    ratio_ref[...] = finish(z_ratio, rt_z)
    drain(ubr, u_recv)

    drain(left_ref, f_recv.at[0])
    drain(right_ref, f_recv.at[1])
    drain(sbuf.at[pl.ds(0, SLOTS - 1)], g_send)
    drain(ubr.at[pl.ds(0, SLOTS - 1)], u_send)
    for cp in swaps:
        cp.wait_send()
    for cp in root_swaps:
        cp.wait_send()
    for i in range(2):
        for q in range(NC):
            @pl.when(jnp.logical_not(is_self(i, q)))
            def _(i=i, q=q):
                drain(rlb.at[pl.ds(0, 8)], root_send.at[0, i, q])
                drain(rrb.at[0, pl.ds(0, half)], root_send.at[1, i, q])
    for n in range(2):
        @pl.when(jnp.logical_not(factor_self(n)))
        def _(n=n):
            drain(lb.at[n], f_send.at[0, n])
            drain(rb.at[n], f_send.at[1, n])


def exchange(block_slot, gradients, adagrad, root_left, root_right):
    vmem = pl.BlockSpec(memory_space=pltpu.VMEM)
    hbm = pl.BlockSpec(memory_space=pl.ANY)
    dma = pltpu.SemaphoreType.DMA
    return pl.pallas_call(
        kernel,
        out_shape=(
            pltpu.VMEM((SLOTS, ROWS, COLS), BF16),
            pltpu.VMEM((2, COLS, WIDTH), BF16),
            pltpu.VMEM((2, COLS, WIDTH), BF16),
            jax.ShapeDtypeStruct((8, 128), F32),
        ),
        in_specs=[hbm] * 5,
        out_specs=(hbm, hbm, hbm, vmem),
        scratch_shapes=[
            pltpu.VMEM((NBLK, ROWS, COLS), BF16),
            pltpu.VMEM((NBLK, ROWS, COLS), F32),
            dma((4,)),
            pltpu.SemaphoreType.REGULAR((2,)),
            pltpu.VMEM((1, NBLK), jnp.int32),
            pltpu.VMEM((8, 128), jnp.int32),
            pltpu.SMEM((8, 128), jnp.int32),
            pltpu.VMEM((SLOTS, ROWS, COLS), BF16),
            pltpu.VMEM((NY, NZ * NX, NC, ROWS, COLS), BF16),
            pltpu.VMEM((NZ * NX, ROWS, WIDTH), BF16),
            pltpu.VMEM((NY, WIDTH, COLS), BF16),
            pltpu.VMEM((WIDTH // 2, WIDTH), BF16),
            pltpu.VMEM((NY, NZ * NX, ROWS, COLS), BF16),
            pltpu.VMEM((2, COLS, WIDTH), BF16),
            pltpu.VMEM((2, COLS, WIDTH), BF16),
            pltpu.VMEM((128, 128), F32),
            pltpu.VMEM((NZ, 8, 128), F32),
            pltpu.VMEM((NX, 8, 128), F32),
            pltpu.VMEM((NY, 8, 128), F32),
            pltpu.VMEM((NC, 2, 8, 128), F32),
            pltpu.VMEM((NZ, 8, 128), F32),
            pltpu.VMEM((NX, 8, 128), F32),
            pltpu.VMEM((NY, 8, 128), F32),
            dma, dma((NY,)), dma((NY,)), dma((NY,)), dma((2, 2, NC)), dma, dma((NY,)),
            dma((NY,)), dma((NY,)), dma((2, 2)), dma((2,)), dma, dma,
            dma((2, NZ)), dma((2, NZ)), dma((2, NX)), dma((2, NX)), dma((2, NY)), dma((2, NY)), dma, dma,
        ],
        compiler_params=pltpu.CompilerParams(
            collective_id=0, has_side_effects=True, vmem_limit_bytes=24 * 2**20
        ),
        cost_estimate=pl.CostEstimate(flops=6 * 10**10, bytes_accessed=6 * 2**20, transcendentals=0),
        name="shampoo_exchange",
    )(*(in_hbm(v) for v in (block_slot.reshape(1, NBLK), gradients, adagrad, root_left, root_right)))


def tail_kernel(
    slot, ratio_v, fl, fr, left, right, g, a, directions, fl_out, fr_out, a_out, upd_out,
    f_buf, a_buf, u_buf, ratio, f_sem, a_sem, u_sem, r_sem,
):
    outs = []

    to_smem = pltpu.make_async_copy(ratio_v, ratio, r_sem)
    to_smem.start()
    parts = 4
    rows = 2 * COLS // parts
    for m, (old, term, out) in enumerate(((fl, left, fl_out), (fr, right, fr_out))):
        for n in range(parts):
            cut = (n * rows // COLS, pl.ds(n * rows % COLS, rows))
            f_buf[(m,) + cut] = 0.9 * old[cut] + 0.1 * term[cut].astype(F32)
            outs.append(pltpu.make_async_copy(f_buf.at[(m,) + cut], out.at[cut], f_sem.at[m, n]))
            outs[-1].start()

    to_smem.wait()

    def scale(b, _):
        t = slot[b]
        u_buf[b] = (directions[t].astype(F32) * ratio[0, t]).astype(BF16)
        return 0

    lax.fori_loop(0, NBLK, scale, 0)
    outs.append(pltpu.make_async_copy(u_buf, upd_out, u_sem))
    outs[-1].start()

    def add(n, _):
        few = pl.ds(n * 4, 4)
        g32 = g[few].astype(F32)
        a_buf[few] = a[few] + g32 * g32
        return 0

    lax.fori_loop(0, NBLK // 4, add, 0)
    outs.append(pltpu.make_async_copy(a_buf, a_out, a_sem))
    outs[-1].start()
    for copy in outs:
        copy.wait()


def tail(block_slot, ratio, factor_left, factor_right, left_term, right_term, gradients, adagrad, directions):
    smem = pl.BlockSpec(memory_space=pltpu.SMEM)
    vmem = pl.BlockSpec(memory_space=pltpu.VMEM)
    hbm = pl.BlockSpec(memory_space=pl.ANY)
    dma = pltpu.SemaphoreType.DMA
    return pl.pallas_call(
        tail_kernel,
        out_shape=(
            jax.ShapeDtypeStruct(factor_left.shape, F32),
            jax.ShapeDtypeStruct(factor_right.shape, F32),
            jax.ShapeDtypeStruct(adagrad.shape, F32),
            jax.ShapeDtypeStruct(gradients.shape, BF16),
        ),
        in_specs=[smem] + [vmem] * 8,
        out_specs=(hbm, hbm, hbm, hbm),
        scratch_shapes=[
            pltpu.VMEM((2, 2, COLS, WIDTH), F32),
            pltpu.VMEM((NBLK, ROWS, COLS), F32),
            pltpu.VMEM((NBLK, ROWS, COLS), BF16),
            pltpu.SMEM((8, 128), F32),
            dma((2, 4)), dma, dma, dma,
        ],
        compiler_params=pltpu.CompilerParams(vmem_limit_bytes=24 * 2**20),
        name="shampoo_tail",
    )(block_slot, ratio, factor_left, factor_right, left_term, right_term, gradients, adagrad, directions)


def on_device(gradients, adagrad, factor_left, factor_right, root_left, root_right, block_slot):
    count = factor_left.shape[0]
    directions, left_term, right_term, ratio = exchange(
        block_slot, gradients, adagrad, root_left.reshape(count, 8, NC, ROWS, WIDTH), root_right
    )
    factor_left_new, factor_right_new, adagrad_new, update = tail(
        block_slot, ratio, factor_left, factor_right, left_term, right_term, gradients, adagrad, directions
    )
    return update, adagrad_new, factor_left_new, factor_right_new


def solution(mesh):
    placed = (
        P(None, "dp", "replica"),
        P(None, "dp", "replica"),
        P("dp", "replica", None),
        P("dp", "replica", None),
        P("dp", "replica", None),
        P("dp", None, "replica"),
        P(),
    )
    return jax.shard_map(
        on_device,
        mesh=mesh,
        in_specs=placed,
        out_specs=(
            P(None, "dp", "replica"),
            P(None, "dp", "replica"),
            P("dp", "replica", None),
            P("dp", "replica", None),
        ),
        check_vma=False,
    )
```

time: 91.5 us -> 89.7 us (0.980); the launches traced: 89.8 us -> 89.6 us
    pallas_call x1, Pallas kernels: 84.1 us -> 85.5 us  [exchange(): pl.pallas_call(kernel, out_shape=(pltpu.VMEM((SLOTS, ROWS, COLS), BF16),...]
    pallas_call x1, Pallas kernels: 4.36 us -> 3.34 us  [tail(): pl.pallas_call(tail_kernel, out_shape=(jax.ShapeDtypeStruct(factor_left.s...]
where the time goes in v4:
time: 89.7 us; the launch traced here: 89.6 us
  Pallas kernels  88.8 us (99%)
    pallas_call x1, Pallas kernels, exchange(): pl.pallas_call(kernel, out_shape=(pltpu.VMEM((SLOTS, ROWS, COLS), BF16),...  85.5 us
    pallas_call x1, Pallas kernels, tail(): pl.pallas_call(tail_kernel, out_shape=(jax.ShapeDtypeStruct(factor_left.s...  3.34 us

profile of v4, /device:TPU:9, one launch (start us, length us, event | category | flops | bytes accessed | tf_op | source)
XLA Modules:
  0.0 89.6 jit_solution(6737347543928465767)
XLA Ops:
  0.6 0.0 copy-start
  0.6 0.0 copy-start.1
  0.7 0.0 copy-start.2
  0.7 0.0 copy-start.3
  0.7 0.0 copy-start.4
  0.7 85.5 %shampoo_exchange.1 = (bf16[128,16,256]{2,1,0:T(8,128)(2,1)S(1)}, bf16[2,256,1024]{2,1,0:T(8,128)(2,1)S(1)}, bf16[2,256,1024]{2,1,0:T(8,128)(2,1)S(1)}, f32[8,128]{1,0:T(8,128)S(1)}) custom-call(s32[1,56]{1,0:T(1,128)} %bitcast.2, bf16[56,16,256]{2,1,0:T(8,128)(2,1)} %g.1, f32[56,16,256]{2,1,0:T(8,128)} %a.1, bf16[2,8,2,16,1024]{4,3,2,1,0:T(8,128)(2,1)} %bitcast.3, ...), custom_call_target="tpu_custom_call" | custom-call | flops 60000002048 | bytes 6291456 | tf_op jit(solution)/shard_map/shampoo_exchange/pallas_call | solution.py:339
  86.2 0.0 copy-done
  86.2 0.0 copy-done.1
  86.2 0.0 copy-done.2
  86.2 0.0 copy-done.3
  86.2 0.0 copy-done.4
  86.2 3.3 %shampoo_tail.1 = (f32[2,256,1024]{2,1,0:T(8,128)}, f32[2,256,1024]{2,1,0:T(8,128)}, f32[56,16,256]{2,1,0:T(8,128)}, bf16[56,16,256]{2,1,0:T(8,128)(2,1)}) custom-call(s32[56]{0:T(128)S(1)} %copy-done.4, f32[8,128]{1,0:T(8,128)S(1)} %get-tuple-element.12.ratio_v, f32[2,256,1024]{2,1,0:T(8,128)S(1)} %copy-done, f32[2,256,1024]{2,1,0:T(8,128)S(1)} %copy-done.1, ...), custom_call_target="tpu_custom_call" | custom-call | tf_op jit(solution)/shard_map/shampoo_tail/pallas_call | solution.py:431
Async XLA Ops:
  0.6 85.6 %copy-start = (f32[2,256,1024]{2,1,0:T(8,128)S(1)}, f32[2,256,1024]{2,1,0:T(8,128)}, u32[]{:S(2)}) copy-start(f32[2,256,1024]{2,1,0:T(8,128)} %fl.1) | copy-start | bytes 6291460
  0.6 85.6 %copy-start.1 = (f32[2,256,1024]{2,1,0:T(8,128)S(1)}, f32[2,256,1024]{2,1,0:T(8,128)}, u32[]{:S(2)}) copy-start(f32[2,256,1024]{2,1,0:T(8,128)} %fr.1) | copy-start | bytes 6291460
  0.7 85.6 %copy-start.2 = (f32[56,16,256]{2,1,0:T(8,128)S(1)}, f32[56,16,256]{2,1,0:T(8,128)}, u32[]{:S(2)}) copy-start(f32[56,16,256]{2,1,0:T(8,128)} %a.1) | copy-start | bytes 2752516
  0.7 85.6 %copy-start.3 = (bf16[56,16,256]{2,1,0:T(8,128)(2,1)S(1)}, bf16[56,16,256]{2,1,0:T(8,128)(2,1)}, u32[]{:S(2)}) copy-start(bf16[56,16,256]{2,1,0:T(8,128)(2,1)} %g.1) | copy-start | bytes 1376260
  0.7 85.6 %copy-start.4 = (s32[56]{0:T(128)S(1)}, s32[56]{0:T(128)}, u32[]{:S(2)}) copy-start(s32[56]{0:T(128)} %slot.1) | copy-start | bytes 676

commit v5 on v4

--- a/solution.py
+++ b/solution.py
@@ -203,28 +203,32 @@
 
     def left_part(n):
         r = 2 * core + n
-        acc = jnp.zeros((COLS, WIDTH), F32)
-        for c in range(NY):
-            rows = gbuf[c, pl.ds(r * 8, 8)].reshape(COLS, COLS)
-            acc = acc + lax.dot_general(
-                rows, gbuf[c].reshape(WIDTH, COLS), (((1,), (1,)), ((), ())), preferred_element_type=F32
-            )
-        lb[n] = acc.astype(BF16)
+        for k in range(NY):
+            acc = jnp.zeros((COLS, COLS), F32)
+            for c in range(NY):
+                acc = acc + lax.dot_general(
+                    gbuf[c, pl.ds(r * 8, 8)].reshape(COLS, COLS),
+                    gbuf[c, pl.ds((r + k) % NY * 8, 8)].reshape(COLS, COLS),
+                    (((1,), (1,)), ((), ())), preferred_element_type=F32,
+                )
+            lb[n, :, k * COLS:(k + 1) * COLS] = acc.astype(BF16)
 
     def right_part(n):
-        cols = gbuf[2 * core + n].reshape(WIDTH, COLS)
-        for c in range(NY):
-            rb[n, :, c * COLS:(c + 1) * COLS] = lax.dot_general(
-                cols, gbuf[c].reshape(WIDTH, COLS), (((0,), (0,)), ((), ())), preferred_element_type=F32
+        r = 2 * core + n
+        for k in range(NY):
+            rb[n, :, k * COLS:(k + 1) * COLS] = lax.dot_general(
+                gbuf[r].reshape(WIDTH, COLS), gbuf[(r + k) % NY].reshape(WIDTH, COLS),
+                (((0,), (0,)), ((), ())), preferred_element_type=F32,
             ).astype(BF16)
 
     def factor_self(n):
         return jnp.logical_and(2 * core + n == y, core == owner)
 
-    def send_factor(m, n, piece):
+    def send_factor(m, n, piece, skip):
         rows = pl.ds(pl.multiple_of(piece * ROWS, ROWS), ROWS)
-        src = (lb, rb)[m].at[n, rows]
-        dst = (left_ref, right_ref)[m].at[i_mine, rows]
+        columns = pl.ds(skip, WIDTH - skip)
+        src = (lb, rb)[m].at[n, rows, columns]
+        dst = (left_ref, right_ref)[m].at[i_mine, rows, columns]
 
         @pl.when(factor_self(n))
         def _():
@@ -234,14 +238,23 @@
         def _():
             remote(src, dst, f_send.at[m, n], f_recv.at[m], device(z, x, owner, 2 * core + n)).start()
 
-    def send_left(piece, _):
-        for n in range(2):
-            send_factor(0, n, piece)
-        return 0
+    def send_terms(m):
+        def upper(piece, _):
+            for n in range(2):
+                send_factor(m, n, piece, 0)
+            return 0
+
+        def lower(piece, _):
+            for n in range(2):
+                send_factor(m, n, piece, COLS // 2)
+            return 0
+
+        lax.fori_loop(0, ROWS // 2, upper, 0)
+        lax.fori_loop(ROWS // 2, ROWS, lower, 0)
 
     for n in range(2):
         left_part(n)
-    lax.fori_loop(0, ROWS, send_left, 0)
+    send_terms(0)
     for n in range(2):
         right_part(n)
 
@@ -301,18 +314,13 @@
     x_ratio = finish(along(1, rt_x, ratio, NX, x_send.at[1], x_recv.at[1]), rt_x)
     y_ratio = along(2, rt_y, x_ratio, NY, y_send.at[1], y_recv.at[1])
 
-    def send_right(piece, _):
-        for n in range(2):
-            send_factor(1, n, piece)
-        return 0
-
-    lax.fori_loop(0, ROWS, send_right, 0)
+    send_terms(1)
     z_ratio = along(0, rt_z, finish(y_ratio, rt_y), NZ, z_send.at[1], z_recv.at[1])
     ratio_ref[...] = finish(z_ratio, rt_z)
     drain(ubr, u_recv)
 
-    drain(left_ref, f_recv.at[0])
-    drain(right_ref, f_recv.at[1])
+    drain(sbuf.at[pl.ds(0, 120)], f_recv.at[0])
+    drain(sbuf.at[pl.ds(0, 120)], f_recv.at[1])
     drain(sbuf.at[pl.ds(0, SLOTS - 1)], g_send)
     drain(ubr.at[pl.ds(0, SLOTS - 1)], u_send)
     for cp in swaps:
@@ -328,8 +336,8 @@
     for n in range(2):
         @pl.when(jnp.logical_not(factor_self(n)))
         def _(n=n):
-            drain(lb.at[n], f_send.at[0, n])
-            drain(rb.at[n], f_send.at[1, n])
+            drain(sbuf.at[pl.ds(0, 60)], f_send.at[0, n])
+            drain(sbuf.at[pl.ds(0, 60)], f_send.at[1, n])
 
 
 def exchange(block_slot, gradients, adagrad, root_left, root_right):
@@ -390,13 +398,21 @@
 
     to_smem = pltpu.make_async_copy(ratio_v, ratio, r_sem)
     to_smem.start()
-    parts = 4
-    rows = 2 * COLS // parts
+    y = lax.axis_index("replica")
+    half = COLS // 2
     for m, (old, term, out) in enumerate(((fl, left, fl_out), (fr, right, fr_out))):
-        for n in range(parts):
-            cut = (n * rows // COLS, pl.ds(n * rows % COLS, rows))
-            f_buf[(m,) + cut] = 0.9 * old[cut] + 0.1 * term[cut].astype(F32)
-            outs.append(pltpu.make_async_copy(f_buf.at[(m,) + cut], out.at[cut], f_sem.at[m, n]))
+        for n in range(4):
+            i, low = n // 2, n % 2
+            rows = pl.ds(low * half, half)
+            for k in range(NY):
+                columns = pl.ds(pl.multiple_of((y + k) % NY * COLS, COLS), COLS)
+                if k == 0 and low:
+                    mirrored = jnp.transpose(term[i, :half, half:COLS].astype(F32))
+                    new = jnp.concatenate([mirrored, term[i, half:, half:COLS].astype(F32)], axis=1)
+                else:
+                    new = term[i, rows, k * COLS:(k + 1) * COLS].astype(F32)
+                f_buf[m, i, rows, columns] = 0.9 * old[i, rows, columns] + 0.1 * new
+            outs.append(pltpu.make_async_copy(f_buf.at[m, i, rows], out.at[i, rows], f_sem.at[m, n]))
             outs[-1].start()
 
     to_smem.wait()

time: 89.7 us -> 89.2 us (level)
  no operation moved by 1% of the time
where the time goes in v5:
time: 89.2 us; the launch traced here: 89.1 us
  Pallas kernels  88.4 us (99%)
    pallas_call x1, Pallas kernels, exchange(): pl.pallas_call(kernel, out_shape=(pltpu.VMEM((SLOTS, ROWS, COLS), BF16),...  84.8 us
    pallas_call x1, Pallas kernels, tail(): pl.pallas_call(tail_kernel, out_shape=(jax.ShapeDtypeStruct(factor_left.s...  3.54 us

profile of v5, /device:TPU:9, one launch (start us, length us, event | category | flops | bytes accessed | tf_op | source)
XLA Modules:
  0.0 89.1 jit_solution(14843797710367874701)
XLA Ops:
  0.6 0.0 copy-start
  0.6 0.0 copy-start.1
  0.7 0.0 copy-start.2
  0.7 0.0 copy-start.3
  0.7 0.0 copy-start.4
  0.7 84.8 %shampoo_exchange.1 = (bf16[128,16,256]{2,1,0:T(8,128)(2,1)S(1)}, bf16[2,256,1024]{2,1,0:T(8,128)(2,1)S(1)}, bf16[2,256,1024]{2,1,0:T(8,128)(2,1)S(1)}, f32[8,128]{1,0:T(8,128)S(1)}) custom-call(s32[1,56]{1,0:T(1,128)} %bitcast.2, bf16[56,16,256]{2,1,0:T(8,128)(2,1)} %g.1, f32[56,16,256]{2,1,0:T(8,128)} %a.1, bf16[2,8,2,16,1024]{4,3,2,1,0:T(8,128)(2,1)} %bitcast.3, ...), custom_call_target="tpu_custom_call" | custom-call | flops 60000002048 | bytes 6291456 | tf_op jit(solution)/shard_map/shampoo_exchange/pallas_call | solution.py:347
  85.5 0.0 copy-done
  85.6 0.0 copy-done.1
  85.6 0.0 copy-done.2
  85.6 0.0 copy-done.3
  85.6 0.0 copy-done.4
  85.6 3.5 %shampoo_tail.1 = (f32[2,256,1024]{2,1,0:T(8,128)}, f32[2,256,1024]{2,1,0:T(8,128)}, f32[56,16,256]{2,1,0:T(8,128)}, bf16[56,16,256]{2,1,0:T(8,128)(2,1)}) custom-call(s32[56]{0:T(128)S(1)} %copy-done.4, f32[8,128]{1,0:T(8,128)S(1)} %get-tuple-element.12.ratio_v, f32[2,256,1024]{2,1,0:T(8,128)S(1)} %copy-done, f32[2,256,1024]{2,1,0:T(8,128)S(1)} %copy-done.1, ...), custom_call_target="tpu_custom_call" | custom-call | tf_op jit(solution)/shard_map/shampoo_tail/pallas_call | solution.py:447
Async XLA Ops:
  0.6 84.9 %copy-start = (f32[2,256,1024]{2,1,0:T(8,128)S(1)}, f32[2,256,1024]{2,1,0:T(8,128)}, u32[]{:S(2)}) copy-start(f32[2,256,1024]{2,1,0:T(8,128)} %fl.1) | copy-start | bytes 6291460
  0.6 84.9 %copy-start.1 = (f32[2,256,1024]{2,1,0:T(8,128)S(1)}, f32[2,256,1024]{2,1,0:T(8,128)}, u32[]{:S(2)}) copy-start(f32[2,256,1024]{2,1,0:T(8,128)} %fr.1) | copy-start | bytes 6291460
  0.7 84.9 %copy-start.2 = (f32[56,16,256]{2,1,0:T(8,128)S(1)}, f32[56,16,256]{2,1,0:T(8,128)}, u32[]{:S(2)}) copy-start(f32[56,16,256]{2,1,0:T(8,128)} %a.1) | copy-start | bytes 2752516
  0.7 84.9 %copy-start.3 = (bf16[56,16,256]{2,1,0:T(8,128)(2,1)S(1)}, bf16[56,16,256]{2,1,0:T(8,128)(2,1)}, u32[]{:S(2)}) copy-start(bf16[56,16,256]{2,1,0:T(8,128)(2,1)} %g.1) | copy-start | bytes 1376260
  0.7 84.9 %copy-start.4 = (s32[56]{0:T(128)S(1)}, s32[56]{0:T(128)}, u32[]{:S(2)}) copy-start(s32[56]{0:T(128)} %slot.1) | copy-start | bytes 676

commit v6 on v5

--- a/solution.py
+++ b/solution.py
@@ -255,8 +255,6 @@
     for n in range(2):
         left_part(n)
     send_terms(0)
-    for n in range(2):
-        right_part(n)
 
     drain(rlb, rl_recv)
     rl = rlb[...].reshape(half, WIDTH)
@@ -304,6 +302,8 @@
     ar_c[core, 1] = finish(y_copies, ar_y)
     c_copy = remote(ar_c.at[core], ar_c.at[core], c_send, c_recv, partner)
     c_copy.start()
+    for n in range(2):
+        right_part(n)
     c_copy.wait()
     search_sq = jnp.sum(ar_c[0, 0] + ar_c[1, 0], keepdims=True)
     graft_all = ar_c[0, 1] + ar_c[1, 1]

time: 89.2 us -> 88.4 us (level)
  Pallas kernels: 88.4 us -> 87.5 us
where the time goes in v6:
time: 88.4 us; the launch traced here: 88.3 us
  Pallas kernels  87.5 us (99%)
    pallas_call x1, Pallas kernels, exchange(): pl.pallas_call(kernel, out_shape=(pltpu.VMEM((SLOTS, ROWS, COLS), BF16),...  84 us
    pallas_call x1, Pallas kernels, tail(): pl.pallas_call(tail_kernel, out_shape=(jax.ShapeDtypeStruct(factor_left.s...  3.54 us

profile of v6, /device:TPU:9, one launch (start us, length us, event | category | flops | bytes accessed | tf_op | source)
XLA Modules:
  0.0 88.3 jit_solution(18209529429221790387)
XLA Ops:
  0.6 0.0 copy-start
  0.6 0.0 copy-start.1
  0.7 0.0 copy-start.2
  0.7 0.0 copy-start.3
  0.7 0.0 copy-start.4
  0.7 84.0 %shampoo_exchange.1 = (bf16[128,16,256]{2,1,0:T(8,128)(2,1)S(1)}, bf16[2,256,1024]{2,1,0:T(8,128)(2,1)S(1)}, bf16[2,256,1024]{2,1,0:T(8,128)(2,1)S(1)}, f32[8,128]{1,0:T(8,128)S(1)}) custom-call(s32[1,56]{1,0:T(1,128)} %bitcast.2, bf16[56,16,256]{2,1,0:T(8,128)(2,1)} %g.1, f32[56,16,256]{2,1,0:T(8,128)} %a.1, bf16[2,8,2,16,1024]{4,3,2,1,0:T(8,128)(2,1)} %bitcast.3, ...), custom_call_target="tpu_custom_call" | custom-call | flops 60000002048 | bytes 6291456 | tf_op jit(solution)/shard_map/shampoo_exchange/pallas_call | solution.py:347
  84.7 0.0 copy-done
  84.7 0.0 copy-done.1
  84.7 0.0 copy-done.2
  84.7 0.0 copy-done.3
  84.7 0.0 copy-done.4
  84.7 3.5 %shampoo_tail.1 = (f32[2,256,1024]{2,1,0:T(8,128)}, f32[2,256,1024]{2,1,0:T(8,128)}, f32[56,16,256]{2,1,0:T(8,128)}, bf16[56,16,256]{2,1,0:T(8,128)(2,1)}) custom-call(s32[56]{0:T(128)S(1)} %copy-done.4, f32[8,128]{1,0:T(8,128)S(1)} %get-tuple-element.12.ratio_v, f32[2,256,1024]{2,1,0:T(8,128)S(1)} %copy-done, f32[2,256,1024]{2,1,0:T(8,128)S(1)} %copy-done.1, ...), custom_call_target="tpu_custom_call" | custom-call | tf_op jit(solution)/shard_map/shampoo_tail/pallas_call | solution.py:447
Async XLA Ops:
  0.6 84.1 %copy-start = (f32[2,256,1024]{2,1,0:T(8,128)S(1)}, f32[2,256,1024]{2,1,0:T(8,128)}, u32[]{:S(2)}) copy-start(f32[2,256,1024]{2,1,0:T(8,128)} %fl.1) | copy-start | bytes 6291460
  0.6 84.1 %copy-start.1 = (f32[2,256,1024]{2,1,0:T(8,128)S(1)}, f32[2,256,1024]{2,1,0:T(8,128)}, u32[]{:S(2)}) copy-start(f32[2,256,1024]{2,1,0:T(8,128)} %fr.1) | copy-start | bytes 6291460
  0.7 84.1 %copy-start.2 = (f32[56,16,256]{2,1,0:T(8,128)S(1)}, f32[56,16,256]{2,1,0:T(8,128)}, u32[]{:S(2)}) copy-start(f32[56,16,256]{2,1,0:T(8,128)} %a.1) | copy-start | bytes 2752516
  0.7 84.1 %copy-start.3 = (bf16[56,16,256]{2,1,0:T(8,128)(2,1)S(1)}, bf16[56,16,256]{2,1,0:T(8,128)(2,1)}, u32[]{:S(2)}) copy-start(bf16[56,16,256]{2,1,0:T(8,128)(2,1)} %g.1) | copy-start | bytes 1376260
  0.7 84.1 %copy-start.4 = (s32[56]{0:T(128)S(1)}, s32[56]{0:T(128)}, u32[]{:S(2)}) copy-start(s32[56]{0:T(128)} %slot.1) | copy-start | bytes 676
